TPU v7x, 256 devices: a whole 4x4x8 slice. The times are simulated.
256 devices in a mesh: lat: 32 (over x, z), mode: 8 (over y, core).
Axes of the slice: x: 4, y: 4, z: 8, core: 2. Of those that a mesh axis runs over, the one named last changes fastest.
Arguments:
- fourier: bfloat16 [8, 48, 3, 1024, 128], P(None, 'mode', None, 'lat'), may hold values from -6 to 6
- wave_table: int32 [32, 2], replicated, may hold values from 0 to 63, as said below
- legendre: bfloat16 [32, 16, 128, 1024], P('lat'), may hold values from -0.1875 to 0.1875
- coupling: float32 [4, 32, 2048], P(None, 'lat'), may hold values from -0.25 to 0.25
- gravity: float32 [48], replicated, may hold values from 0.5 to 40
- hyper_diff: float32 [48], replicated, may hold values from 0.5 to 20
- strata_into_eigenbasis: float32 [48, 48], replicated, may hold values from -0.875 to 0.875
- vertical_out: float32 [48, 48], replicated, may hold values from -0.875 to 0.875
Outputs:
- fourier_new: bfloat16 [8, 48, 3, 1024, 128], P(None, 'mode', None, 'lat')
Inputs may be any that keep to these rules, and one draw needn't show every extreme that they name: `wave_table`: every window index appears exactly once. In each row, entries 2 s and 2 s + 1 are w and 63 - w for some w.
All inputs are finite; a program needn't handle non-finite values.
Results may differ from a plain program's by a relative error of at most 0.0047.
Values may be sent and summed in bfloat16 or wider, within the bound.
No kernel may reach another device: no remote copies, remote signals or barrier semaphores. Data moves between devices by JAX's collectives and lax.ppermute only.
A program may use at most 128 MiB of HBM per device.

v0:
```python
import jax
import jax.numpy as jnp
from jax import lax
from jax.sharding import PartitionSpec as P

NN = 1792
BLK = 128
SWEEPS = 3


def pack_layout(row_waves, window, degrees, block_rows):
    blocks = degrees // block_rows
    per_pair = blocks + 2
    pair_total = row_waves.shape[0] // 2
    lowest = row_waves * degrees // window
    first_block = lowest // block_rows
    counts = blocks - first_block
    rows_all = jnp.arange(pair_total * per_pair * block_rows, dtype=jnp.int32)
    within = rows_all % block_rows
    block_pos = rows_all // block_rows
    pair_slot = block_pos // per_pair
    offset = block_pos % per_pair
    lead_slot = 2 * pair_slot
    lead_count = jnp.take(counts, lead_slot)
    trail_count = jnp.take(counts, lead_slot + 1)
    in_lead = offset < lead_count
    in_trail = jnp.logical_and(jnp.logical_not(in_lead), offset < lead_count + trail_count)
    member = jnp.where(in_lead, lead_slot, lead_slot + 1)
    degree_block = jnp.where(
        in_lead,
        jnp.take(first_block, lead_slot) + offset,
        jnp.take(first_block, lead_slot + 1) + offset - lead_count,
    )
    degree = degree_block * block_rows + within
    usable = jnp.logical_and(jnp.logical_or(in_lead, in_trail), degree >= jnp.take(lowest, member))
    degree = jnp.where(usable, degree, 0)
    return (member, degree, usable)


def shifted(values, distance):
    filler = jnp.zeros(values.shape[:-1] + (abs(distance),), values.dtype)
    if distance > 0:
        return jnp.concatenate([values[..., distance:], filler], axis=-1)
    return jnp.concatenate([filler, values[..., :distance]], axis=-1)


def solve_modes(
    spectral,
    member,
    degree,
    usable,
    coupling,
    gravity,
    hyper_diff,
    strata_into_eigenbasis,
    vertical_out,
):
    state_tensors = spectral.astype(jnp.float32)
    vorticity = state_tensors[:, :, 0]
    divergence = state_tensors[:, :, 1]
    thermal_state = state_tensors[:, :, 2]
    wave_factor = (degree * (degree + 1)).astype(jnp.float32) / float(NN * NN)
    highest = lax.Precision.HIGHEST
    div_modes = jnp.einsum("kl,elpr->ekpr", strata_into_eigenbasis, divergence, precision=highest)
    temp_modes = jnp.einsum(
        "kl,elpr->ekpr", strata_into_eigenbasis, thermal_state, precision=highest
    )
    source_side = div_modes - wave_factor * temp_modes
    link_weights = []
    for index, distance in enumerate((-2, -1, 1, 2)):
        joined = jnp.logical_and(
            jnp.logical_and(usable, shifted(usable, distance)), member == shifted(member, distance)
        )
        link_weights.append(jnp.where(joined, coupling[index], 0.0))
    gravity_wide = gravity[None, :, None, None]
    diagonal = 1.0 + gravity_wide * wave_factor
    answer = jnp.zeros_like(source_side)
    for repeat in range(SWEEPS):
        beside_all = link_weights[0] * shifted(answer, -2)
        beside_all = beside_all + link_weights[1] * shifted(answer, -1)
        beside_all = beside_all + link_weights[2] * shifted(answer, 1)
        beside_all = beside_all + link_weights[3] * shifted(answer, 2)
        applied = answer + gravity_wide * wave_factor * (answer + beside_all)
        answer = answer + (source_side - applied) / diagonal
    temp_new = temp_modes - 0.5 * answer
    vort_new = vorticity / (1.0 + hyper_diff[None, :, None, None] * wave_factor * wave_factor)
    div_out = jnp.einsum("lk,ekpr->elpr", vertical_out, answer, precision=highest)
    temp_out = jnp.einsum("lk,ekpr->elpr", vertical_out, temp_new, precision=highest)
    result = jnp.stack([vort_new, div_out, temp_out], axis=2)
    result = jnp.where(usable, result, 0.0)
    return result.astype(jnp.bfloat16)


def to_spectral(tables, at_owner, member_block, usable):
    slots, nlat = (at_owner.shape[0], at_owner.shape[-1])
    flat = at_owner.reshape(slots, -1, nlat)
    block_rows = tables.shape[1]
    rows = tables.shape[0] * block_rows

    def to_one_block(index, total):
        index = jnp.asarray(index).astype(jnp.int32)
        table = lax.dynamic_index_in_dim(tables, index, 0, keepdims=False)
        picked = lax.dynamic_index_in_dim(flat, member_block[index], 0, keepdims=False)
        term = jnp.einsum("nl,cl->cn", table, picked, preferred_element_type=jnp.float32)
        return lax.dynamic_update_slice_in_dim(total, term, index * block_rows, 1)

    total = lax.fori_loop(
        0, tables.shape[0], to_one_block, jnp.zeros((flat.shape[1], rows), jnp.float32)
    )
    spectral = total.reshape(at_owner.shape[1:5] + (rows,))
    return jnp.where(usable, spectral, 0.0).astype(jnp.bfloat16)


def synthesise_grid(tables, updated, member_block, slots):
    rows = updated.shape[-1]
    flat = updated.reshape(-1, rows)
    block_rows = tables.shape[1]

    def synthesise_one_block(index, total):
        index = jnp.asarray(index).astype(jnp.int32)
        table = lax.dynamic_index_in_dim(tables, index, 0, keepdims=False)
        values = lax.dynamic_slice_in_dim(flat, index * block_rows, block_rows, 1)
        term = jnp.einsum("nl,cn->cl", table, values, preferred_element_type=jnp.float32)
        slot = member_block[index]
        current = lax.dynamic_index_in_dim(total, slot, 0, keepdims=False)
        return lax.dynamic_update_index_in_dim(total, current + term, slot, 0)

    start = jnp.zeros((slots, flat.shape[0], tables.shape[2]), jnp.float32)
    total = lax.fori_loop(0, tables.shape[0], synthesise_one_block, start)
    return total.astype(jnp.bfloat16)


def body(
    fourier,
    wave_table,
    legendre,
    coupling,
    gravity,
    hyper_diff,
    strata_into_eigenbasis,
    vertical_out,
):
    window = fourier.shape[4] // 2
    split_parts = fourier.reshape(fourier.shape[:4] + (2, window))
    wave_order = wave_table.reshape(-1)
    inverse_order = (
        jnp.zeros((window,), jnp.int32).at[wave_order].set(jnp.arange(window, dtype=jnp.int32))
    )
    row_waves = lax.dynamic_index_in_dim(wave_table, lax.axis_index("lat"), 0, keepdims=False)
    member, degree, usable = pack_layout(row_waves, window, NN, BLK)
    member_block = member.reshape(-1, BLK)[:, 0]
    tables = legendre[0]
    link_terms = coupling[:, 0]
    sending = jnp.transpose(jnp.take(split_parts, wave_order, axis=5), (5, 0, 1, 2, 4, 3))
    at_owner = lax.all_to_all(
        lax.all_to_all(sending, "lat", split_axis=0, concat_axis=5, tiled=True),
        "mode",
        split_axis=1,
        concat_axis=2,
        tiled=True,
    )
    spectral = to_spectral(tables, at_owner, member_block, usable)
    updated = solve_modes(
        spectral,
        member,
        degree,
        usable,
        link_terms,
        gravity,
        hyper_diff,
        strata_into_eigenbasis,
        vertical_out,
    )
    synthesis = synthesise_grid(tables, updated, member_block, at_owner.shape[0])
    returned = lax.all_to_all(
        lax.all_to_all(
            synthesis.reshape(at_owner.shape), "lat", split_axis=5, concat_axis=0, tiled=True
        ),
        "mode",
        split_axis=2,
        concat_axis=1,
        tiled=True,
    )
    restored = jnp.take(returned, inverse_order, axis=0)
    ordered = jnp.transpose(restored, (1, 2, 3, 5, 4, 0))
    return ordered.reshape(fourier.shape)


def solution(mesh):
    placed = (
        P(None, "mode", None, "lat", None),
        P(),
        P("lat", None, None, None),
        P(None, "lat", None),
        P(),
        P(),
        P(),
        P(),
    )
    return jax.shard_map(
        body,
        mesh=mesh,
        in_specs=placed,
        out_specs=P(None, "mode", None, "lat", None),
        check_vma=False,
    )
```

profile of v0, /device:TPU:1, one launch (start us, length us, event | category | flops | bytes accessed | tf_op | source)
XLA Modules:
  0.0 386.1 jit_solution(2665013349996031129)
XLA Ops:
  1.0 4.2 %reshape.267 = bf16[8,6,3,32,2,64]{5,4,3,2,1,0:T(2,128)(2,1)S(1)} reshape(bf16[8,6,3,32,128]{4,3,2,1,0:T(8,128)(2,1)} %param.14) | data formatting | bytes 2359296 | tf_op jit(solution)/shard_map/reshape | solution.py:144
  5.2 8.0 %copy.58 = bf16[8,6,3,32,2,64]{3,0,4,2,1,5:T(8,128)(2,1)} copy(bf16[8,6,3,32,2,64]{5,4,3,2,1,0:T(2,128)(2,1)S(1)} %reshape.267) | data formatting | bytes 2359296 | tf_op jit(solution)/shard_map/reshape | solution.py:144
  13.2 5.7 %gather_fusion = bf16[64,8,6,3,32,2]{4,1,5,3,2,0:T(8,128)(2,1)} fusion(bf16[8,6,3,32,2,64]{3,0,4,2,1,5:T(8,128)(2,1)} %copy.58, s32[1024]{0:T(1024)S(1)} %pad_clamp_fusion.1), kind=kCustom, calls=%fused_computation | custom fusion | bytes 2359552 | tf_op jit(solution)/shard_map/jit(_take)/gather | solution.py:154
  18.9 5.0 %fusion.76 = bf16[64,6,3,2,8,32]{5,4,3,2,1,0:T(8,128)(2,1)} fusion(bf16[64,8,6,3,32,2]{4,1,5,3,2,0:T(8,128)(2,1)} %gather_fusion, pred[64]{0:T(512)(128)(4,1)S(1)} %compare_and_fusion.2), kind=kLoop, calls=%fused_computation.142 | loop fusion | flops 589824 | bytes 2359360
  23.9 7.9 %reshape.368 = bf16[32,2,9216]{2,1,0:T(2,128)(2,1)} reshape(bf16[64,6,3,2,8,32]{5,4,3,2,1,0:T(8,128)(2,1)} %fusion.76) | data formatting | bytes 2359296
  31.7 12.0 %all-to-all-start = ((bf16[32,2,9216]{2,1,0:T(2,128)(2,1)}), bf16[32,2,9216]{2,1,0:T(2,128)(2,1)S(1)}, u32[]{:S(2)}, u32[]{:S(2)}) async-start(bf16[32,2,9216]{2,1,0:T(2,128)(2,1)} %reshape.368), calls=%async_computation | async-start | bytes 2359296 | tf_op jit(solution)/shard_map/all_to_all | solution.py:156
  45.2 3.8 fusion.47
  49.1 1.3 add_select_fusion.3
  50.4 1.3 fusion.55
  52.1 19.2 %all-to-all-done = bf16[32,2,9216]{2,1,0:T(2,128)(2,1)S(1)} async-done(((bf16[32,2,9216]{2,1,0:T(2,128)(2,1)}), bf16[32,2,9216]{2,1,0:T(2,128)(2,1)S(1)}, u32[]{:S(2)}, u32[]{:S(2)}) %all-to-all-start) | async-done | bytes 1179680 | tf_op jit(solution)/shard_map/all_to_all | solution.py:156
  71.3 3.8 reshape.369
  75.0 7.6 %copy.72 = bf16[2,8,6,3,2,32,32]{6,5,4,3,2,0,1:T(8,128)(2,1)} copy(bf16[2,8,6,3,2,32,32]{6,1,4,3,2,0,5:T(8,128)(2,1)} %bitcast.126) | data formatting | bytes 2359296 | tf_op jit(solution)/shard_map/all_to_all | solution.py:156
  82.6 7.9 %reshape.363 = bf16[2,8,6,3,2,1024]{5,4,3,2,0,1:T(2,128)(2,1)} reshape(bf16[2,8,6,3,2,32,32]{6,5,4,3,2,0,1:T(8,128)(2,1)} %copy.72) | data formatting | bytes 2359296 | tf_op jit(solution)/shard_map/all_to_all | solution.py:156
  90.6 9.4 %all-to-all-start.1 = ((bf16[2,8,6,3,2,1024]{5,4,3,2,0,1:T(2,128)(2,1)}), bf16[2,8,6,3,2,1024]{5,4,3,2,0,1:T(2,128)(2,1)S(1)}, u32[]{:S(2)}, u32[]{:S(2)}) async-start(bf16[2,8,6,3,2,1024]{5,4,3,2,0,1:T(2,128)(2,1)} %reshape.363), calls=%async_computation.1 | async-start | bytes 2359296 | tf_op jit(solution)/shard_map/all_to_all | solution.py:155
  99.9 3.9 fusion.30
  103.9 3.9 %multiply_add_fusion.1 = (f32[2048]{0:T(1024)S(1)}, f32[2048]{0:T(1024)S(1)}, f32[2048]{0:T(1024)S(1)}, f32[2048]{0:T(1024)S(1)}, f32[2048]{0:T(1024)S(1)}) fusion(f32[2046]{0:T(1024)S(1)} %broadcast.301, f32[2047]{0:T(1024)S(1)} %broadcast.300, f32[2]{0:T(128)S(1)} %broadcast.299, f32[2048]{0:T(1024)S(1)} %bitcast.138, s32[2046]{0:T(1024)S(1)} %get-tuple-element.255, ...), kind=kLoop, calls=%fused_computation.87 | loop fusion | flops 217088 | bytes 131067 | tf_op jit(solution)/shard_map/add | solution.py:82
  108.7 7.8 %all-to-all-done.1 = bf16[2,8,6,3,2,1024]{5,4,3,2,0,1:T(2,128)(2,1)S(1)} async-done(((bf16[2,8,6,3,2,1024]{5,4,3,2,0,1:T(2,128)(2,1)}), bf16[2,8,6,3,2,1024]{5,4,3,2,0,1:T(2,128)(2,1)S(1)}, u32[]{:S(2)}, u32[]{:S(2)}) %all-to-all-start.1) | async-done | bytes 1179680 | tf_op jit(solution)/shard_map/all_to_all | solution.py:155
  118.0 61.9 %while.26 = (s32[]{:T(128)}, bf16[288,2048]{1,0:T(8,128)(2,1)S(1)}, s32[16]{0:T(128)S(1)}, bf16[2,288,1024]{2,1,0:T(8,128)(2,1)S(1)}, bf16[16,128,1024]{2,1,0:T(...) while((s32[]{:T(128)}, bf16[288,2048]{1,0:T(8,128)(2,1)S(1)}, ...), condition=%wide.region_2.4_spmd, body=%wide.region_1.3_spmd.sunk | while | flops 75497480 | bytes 1000137 | solution.py:107
  120.5 1.3 convolution_dynamic-update-slice_fusion.2
  128.3 1.3 convolution_dynamic-update-slice_fusion.2
  132.1 1.3 convolution_dynamic-update-slice_fusion.2
  136.0 1.3 convolution_dynamic-update-slice_fusion.2
  143.7 1.3 convolution_dynamic-update-slice_fusion.2
  147.6 1.3 convolution_dynamic-update-slice_fusion.2
  151.5 1.3 convolution_dynamic-update-slice_fusion.2
  159.2 1.3 convolution_dynamic-update-slice_fusion.2
  163.1 1.3 convolution_dynamic-update-slice_fusion.2
  166.9 1.3 convolution_dynamic-update-slice_fusion.2
  174.7 1.3 convolution_dynamic-update-slice_fusion.2
  178.5 1.3 convolution_dynamic-update-slice_fusion.2
  190.1 63.8 %while.27 = (s32[]{:T(128)}, f32[2,288,1024]{2,1,0:T(8,128)S(1)}, s32[16]{0:T(128)S(1)}, bf16[288,2048]{1,0:T(8,128)(2,1)}, bf16[16,128,1024]{2,1,0:T(8,128)(2,1...) while((s32[]{:T(128)}, f32[2,288,1024]{2,1,0:T(8,128)S(1)}, s32[16]{0:T(128)S(1)}, ...), condition=%wide.region_4.6_spmd, body=%wide.region_3.5_spmd.sunk | while | flops 75792392 | bytes 5055181 | solution.py:129
  254.0 2.2 copy.65
  256.3 8.4 %copy.66 = bf16[2,1,48,3,2,1024]{2,4,3,0,1,5:T(2,128)(2,1)S(1)} copy(bf16[2,1,48,3,2,1024]{5,0,4,3,2,1:T(2,128)(2,1)} %bitcast.134) | data formatting | bytes 2359296 | tf_op jit(solution)/shard_map/reshape | solution.py:177
  264.7 5.4 %reshape.370 = bf16[32,2,9216]{2,1,0:T(2,128)(2,1)} reshape(bf16[1024,1,2,3,2,48]{5,4,3,2,1,0:T(2,128)(2,1)S(1)} %bitcast.128) | data formatting | bytes 2359296
  270.1 35.0 %all_to_all.57 = bf16[32,2,9216]{2,1,0:T(2,128)(2,1)} all-to-all(bf16[32,2,9216]{2,1,0:T(2,128)(2,1)} %reshape.370), channel_id=1, replica_groups=mesh['lat'=32,'mode'=8] {'lat'}, dimensions={0} | all-to-all | bytes 2359296 | tf_op jit(solution)/shard_map/all_to_all | solution.py:176
  305.1 4.2 %reshape.371 = bf16[1024,1,2,3,2,48]{5,4,3,2,1,0:T(2,128)(2,1)S(1)} reshape(bf16[32,2,9216]{2,1,0:T(2,128)(2,1)} %all_to_all.57) | data formatting | bytes 2359296
  309.3 8.4 %copy.73 = bf16[2,1,48,3,2,32,32]{6,5,2,4,3,0,1:T(8,128)(2,1)} copy(bf16[2,1,48,3,2,32,32]{2,4,3,0,6,5,1:T(2,128)(2,1)S(1)} %bitcast.129) | data formatting | bytes 2359296 | tf_op jit(solution)/shard_map/all_to_all | solution.py:176
  317.7 6.8 %copy.68 = bf16[32,2,1,48,3,2,32]{3,6,5,4,1,0,2:T(8,128)(2,1)S(1)} copy(bf16[32,2,1,48,3,2,32]{6,0,3,5,4,1,2:T(8,128)(2,1)} %bitcast.127) | data formatting | bytes 2359296 | tf_op jit(solution)/shard_map/all_to_all | solution.py:176
  324.4 4.9 %copy.69 = bf16[64,1,48,3,2,32]{0,5,4,3,1,2:T(8,128)(2,1)} copy(bf16[64,1,48,3,2,32]{2,5,4,3,0,1:T(8,128)(2,1)S(1)} %bitcast.130) | data formatting | bytes 2359296 | tf_op jit(solution)/shard_map/all_to_all | solution.py:176
  329.3 4.5 %reshape.372 = bf16[8,2,36864]{2,1,0:T(2,128)(2,1)} reshape(bf16[48,1,3,2,32,64]{5,4,3,2,1,0:T(8,128)(2,1)} %bitcast.132) | data formatting | bytes 2359296
  333.8 7.4 %all-to-all-start.3 = ((bf16[8,2,36864]{2,1,0:T(2,128)(2,1)}), bf16[8,2,36864]{2,1,0:T(2,128)(2,1)S(1)}, u32[]{:S(2)}, u32[]{:S(2)}) async-start(bf16[8,2,36864]{2,1,0:T(2,128)(2,1)} %reshape.372), calls=%async_computation.3 | async-start | bytes 2359296 | tf_op jit(solution)/shard_map/all_to_all | solution.py:175
  342.1 15.7 %all-to-all-done.3 = bf16[8,2,36864]{2,1,0:T(2,128)(2,1)S(1)} async-done(((bf16[8,2,36864]{2,1,0:T(2,128)(2,1)}), bf16[8,2,36864]{2,1,0:T(2,128)(2,1)S(1)}, u32[]{:S(2)}, u32[]{:S(2)}) %all-to-all-start.3) | async-done | bytes 1179680 | tf_op jit(solution)/shard_map/all_to_all | solution.py:175
  357.8 1.6 reshape.373
  359.3 5.2 %copy.70 = bf16[64,8,6,3,2,32]{5,1,4,3,2,0:T(8,128)(2,1)} copy(bf16[64,8,6,3,2,32]{0,5,4,3,2,1:T(8,128)(2,1)S(1)} %bitcast.131) | data formatting | bytes 2359296 | tf_op jit(solution)/shard_map/all_to_all | solution.py:175
  364.5 5.7 %gather_fusion.1 = bf16[64,8,6,3,2,32]{5,1,4,3,2,0:T(8,128)(2,1)} fusion(bf16[64,8,6,3,2,32]{5,1,4,3,2,0:T(8,128)(2,1)} %copy.70, s32[1024]{0:T(1024)S(1)} %pad_clamp_fusion), kind=kCustom, calls=%fused_computation.1 | custom fusion | bytes 2359552 | tf_op jit(solution)/shard_map/jit(_take)/gather | solution.py:184
  370.2 5.0 %select_bitcast_fusion.1 = bf16[8,6,3,32,2,64]{3,0,4,2,1,5:T(8,128)(2,1)} fusion(bf16[64,8,6,3,2,32]{5,1,4,3,2,0:T(8,128)(2,1)} %gather_fusion.1, pred[64]{0:T(512)(128)(4,1)S(1)} %compare_and_fusion.3), kind=kLoop, calls=%fused_computation.18 | loop fusion | flops 589824 | bytes 2359360 | tf_op jit(solution)/shard_map/jit(_take)/select_n | solution.py:184
  375.2 8.7 %copy.71 = bf16[8,6,3,32,2,64]{5,4,3,2,1,0:T(2,128)(2,1)S(1)} copy(bf16[8,6,3,32,2,64]{3,0,4,2,1,5:T(8,128)(2,1)} %select_bitcast_fusion.1) | data formatting | bytes 2359296 | tf_op jit(solution)/shard_map/jit(_take)/select_n | solution.py:184
  383.9 2.2 reshape.275
  (131 shorter events, 64.2 us)
Async XLA Ops:
  0.0 181.2 %copy-start = (f32[48,48]{1,0:T(8,128)S(1)}, f32[48,48]{1,0:T(8,128)}, u32[]{:S(2)}) copy-start(f32[48,48]{1,0:T(8,128)} %param.20) | copy-start | bytes 27652
  31.7 12.0 %copy-start.5 = (s32[32,2]{0,1:T(2,128)S(1)}, s32[32,2]{0,1:T(2,128)}, u32[]{:S(2)}) copy-start(s32[32,2]{0,1:T(2,128)} %param.15) | copy-start | bytes 772
  31.7 20.3 %copy-start.4 = (f32[4,1,2048]{2,1,0:T(1,128)S(1)}, f32[4,1,2048]{2,1,0:T(1,128)}, u32[]{:S(2)}) copy-start(f32[4,1,2048]{2,1,0:T(1,128)} %param.17) | copy-start | bytes 98308
  31.7 39.5 %all-to-all-start = ((bf16[32,2,9216]{2,1,0:T(2,128)(2,1)}), bf16[32,2,9216]{2,1,0:T(2,128)(2,1)S(1)}, u32[]{:S(2)}, u32[]{:S(2)}) async-start(bf16[32,2,9216]{2,1,0:T(2,128)(2,1)} %reshape.368), calls=%async_computation | async-start | bytes 2359296 | tf_op jit(solution)/shard_map/all_to_all | solution.py:156
  90.5 17.2 %copy-start.6 = (f32[48]{0:T(128)S(1)}, f32[48]{0:T(128)}, u32[]{:S(2)}) copy-start(f32[48]{0:T(128)} %param.18) | copy-start | bytes 580
  90.6 17.2 %copy-start.7 = (f32[48]{0:T(128)S(1)}, f32[48]{0:T(128)}, u32[]{:S(2)}) copy-start(f32[48]{0:T(128)} %param.19) | copy-start | bytes 580
  90.6 25.9 %all-to-all-start.1 = ((bf16[2,8,6,3,2,1024]{5,4,3,2,0,1:T(2,128)(2,1)}), bf16[2,8,6,3,2,1024]{5,4,3,2,0,1:T(2,128)(2,1)S(1)}, u32[]{:S(2)}, u32[]{:S(2)}) async-start(bf16[2,8,6,3,2,1024]{5,4,3,2,0,1:T(2,128)(2,1)} %reshape.363), calls=%async_computation.1 | async-start | bytes 2359296 | tf_op jit(solution)/shard_map/all_to_all | solution.py:155
  184.1 0.7 copy-start.3
  184.9 1.7 copy-start.2
  333.8 23.9 %all-to-all-start.3 = ((bf16[8,2,36864]{2,1,0:T(2,128)(2,1)}), bf16[8,2,36864]{2,1,0:T(2,128)(2,1)S(1)}, u32[]{:S(2)}, u32[]{:S(2)}) async-start(bf16[8,2,36864]{2,1,0:T(2,128)(2,1)} %reshape.372), calls=%async_computation.3 | async-start | bytes 2359296 | tf_op jit(solution)/shard_map/all_to_all | solution.py:175
  375.2 10.9 %copy-start.1 = (f32[48,48]{1,0:T(8,128)S(1)}, f32[48,48]{1,0:T(8,128)}, u32[]{:S(2)}) copy-start(f32[48,48]{1,0:T(8,128)} %param.20) | copy-start | bytes 27652
where the time goes:
time: 390 us; the launch traced here: 386 us
  local copies, waits for them, and re-layouts  144 us (37%)
  loops' own time  62.1 us (16%)
  matrix products  44.5 us (11%)
  waiting for transfers between devices  42.7 us (11%)
  blocking collectives  35 us (9%)
  other arithmetic  28.9 us (7%)
  starting transfers between devices  28.8 us (7%)
    all_to_all x1, blocking collectives, body(): lax.all_to_all(synthesis.reshape(at_owner.shape), 'lat', split_axis=5, co...  35 us
    another operation x1, loops' own time, to_spectral(): lax.fori_loop(0, tables.shape[0], to_one_block, jnp.zeros((flat.shape[1],...  31.5 us
    another operation x1, loops' own time, synthesise_grid(): total = lax.fori_loop(0, tables.shape[0], synthesise_one_block, start)  30.6 us
    unnamed x23, local copies, waits for them, and re-layouts  28.2 us
    dot_general x16, matrix products, to_one_block(): jnp.einsum('nl,cl->cn', table, picked, preferred_element_type=jnp.float32)  20.9 us
    dot_general x16, matrix products, synthesise_one_block(): jnp.einsum('nl,cn->cl', table, values, preferred_element_type=jnp.float32)  20.9 us
    all_to_all x3, local copies, waits for them, and re-layouts, body(): lax.all_to_all(synthesis.reshape(at_owner.shape), 'lat', split_axis=5, co...  20 us
    all_to_all x1, waiting for transfers between devices, body(): lax.all_to_all(sending, 'lat', split_axis=0, concat_axis=5, tiled=True)  19.2 us
  transfers between devices with their start and end apart: 3, of which 3 were waited for; matrix products, arithmetic and copies ran while one was open for 5% of the time, Pallas kernels for 0%

commit v1 on v0

v1 whole, which is shorter than its diff:
```python
import functools

import jax
import jax.numpy as jnp
from jax import lax
from jax.experimental import pallas as pl
from jax.experimental.pallas import tpu as pltpu
from jax.sharding import PartitionSpec as P

NN = 1792
BLK = 128
SWEEPS = 3
LANES = 128
BAND = 32
F32 = jnp.float32
BF16 = jnp.bfloat16


def swap_blocks(parts):
    y0, y1, y2, y3 = parts
    lane = lax.broadcasted_iota(jnp.int32, y0.shape, 1)
    low = lane < 64
    n0 = jnp.where(low, y0, pltpu.roll(y2, 64, 1))
    n2 = jnp.where(low, pltpu.roll(y0, 64, 1), y2)
    n1 = jnp.where(low, y1, pltpu.roll(y3, 64, 1))
    n3 = jnp.where(low, pltpu.roll(y1, 64, 1), y3)
    even = (lane & 32) == 0
    z0 = jnp.where(even, n0, pltpu.roll(n1, 32, 1))
    z1 = jnp.where(even, pltpu.roll(n0, 96, 1), n1)
    z2 = jnp.where(even, n2, pltpu.roll(n3, 32, 1))
    z3 = jnp.where(even, pltpu.roll(n2, 96, 1), n3)
    return z0, z1, z2, z3


def wave_selector(table_ref, owners, window):
    lane = lax.broadcasted_iota(jnp.int32, (owners, LANES), 1)
    rows = []
    for slot in range(2):
        for part in range(2):
            rows.append(jnp.where(table_ref[:, slot : slot + 1] + part * window == lane, 1.0, 0.0))
    return jnp.concatenate(rows, axis=0).astype(BF16)


def pack_kernel(table_ref, x_ref, out_ref, stage_ref, *, owners, window):
    selector = wave_selector(table_ref, owners, window)
    columns = x_ref.shape[0] // BAND
    for pair in range(columns // 8):
        both = lax.dot_general(
            selector,
            x_ref[pair * 256 : (pair + 1) * 256, :],
            (((1,), (1,)), ((), ())),
            preferred_element_type=F32,
        )
        for half in range(2):
            turned = both[:, half * 128 : (half + 1) * 128]
            parts = swap_blocks([turned[i * owners : (i + 1) * owners] for i in range(4)])
            for i in range(4):
                stage_ref[pl.ds(pair * 8 + half * 4 + i, owners, stride=columns), :] = parts[i]
    out_ref[...] = stage_ref[...].astype(BF16)


def unpack_kernel(table_ref, x_ref, out_ref, stage_ref, *, owners, window):
    selector = wave_selector(table_ref, owners, window)
    columns = out_ref.shape[0] // BAND
    stage_ref[...] = x_ref[...].astype(F32)
    for group in range(columns // 4):
        parts = [stage_ref[pl.ds(group * 4 + i, owners, stride=columns), :] for i in range(4)]
        turned = jnp.concatenate(swap_blocks(parts), axis=0).astype(BF16)
        rows = lax.dot_general(
            turned, selector, (((0,), (0,)), ((), ())), preferred_element_type=F32
        )
        out_ref[group * 128 : (group + 1) * 128, :] = rows.astype(BF16)


def layout_at(index, waves, window):
    blocks = NN // BLK
    low0, low1 = (waves[0] * NN) // window, (waves[1] * NN) // window
    first0, first1 = low0 // BLK, low1 // BLK
    count0, count1 = blocks - first0, blocks - first1
    block = index >> 7
    lead = block < count0
    held = jnp.logical_and(index >= 0, block < count0 + count1)
    degree = jnp.where(lead, first0 * BLK, (first1 - count0) * BLK) + index
    usable = jnp.logical_and(held, degree >= jnp.where(lead, low0, low1))
    return lead, jnp.where(usable, degree, 0), usable


def split(values):
    high = values.astype(BF16)
    return high, (values - high.astype(F32)).astype(BF16)


def column_of(row, size):
    diagonal = lax.broadcasted_iota(jnp.int32, (size, size), 0) == lax.broadcasted_iota(
        jnp.int32, (size, size), 1
    )
    return jnp.sum(jnp.where(diagonal, row, 0.0), axis=1, keepdims=True)


def owner_kernel(
    me_ref,
    table_ref,
    q_ref,
    legendre_ref,
    coupling_ref,
    gravity_ref,
    hyper_ref,
    into_ref,
    out_of_ref,
    out_ref,
    grid_ref,
    spec_ref,
    right_ref,
    temp_ref,
    scale_ref,
    links_ref,
    update_ref,
    total_ref,
    *,
    window,
    levels,
):
    rows = legendre_ref.shape[0]
    owners = q_ref.shape[0] // (3 * levels)
    cols = 3 * levels
    waves = (table_ref[me_ref[0], 0], table_ref[me_ref[0], 1])
    count0 = NN // BLK - (waves[0] * NN) // window // BLK
    straddles = count0 % 2 == 1
    cut = pl.multiple_of(count0 * BLK, BLK)

    index = lax.broadcasted_iota(jnp.int32, (8, rows), 1)
    lead, degree, usable = layout_at(index, waves, window)
    wave_factor = (degree * (degree + 1)).astype(F32) / float(NN * NN)
    usable_f = jnp.where(usable, 1.0, 0.0)
    for number, distance in enumerate((-2, -1, 1, 2)):
        other_lead, _, other_usable = layout_at(index + distance, waves, window)
        joined = jnp.logical_and(jnp.logical_and(usable, other_usable), lead == other_lead)
        inside = jnp.logical_and(index + distance >= 0, index + distance < rows)
        joined = jnp.logical_and(joined, inside)
        links_ref[number] = jnp.where(joined, coupling_ref[number : number + 1, :], 0.0)
    gravity = column_of(gravity_ref[...], levels)
    weighted = gravity * wave_factor[:1]
    inverse = 1.0 / (1.0 + weighted)
    scale_ref[...] = weighted * inverse

    spread_row = lax.broadcasted_iota(jnp.int32, (levels, cols), 0)
    spread_col = lax.broadcasted_iota(jnp.int32, (levels, cols), 1)
    tall_row = lax.broadcasted_iota(jnp.int32, (cols, levels), 0)
    tall_col = lax.broadcasted_iota(jnp.int32, (cols, levels), 1)
    into_parts = split(into_ref[...])
    out_parts = split(out_of_ref[...])
    mix_in, mix_out = [], []
    for part in range(2):
        for field in (1, 2):
            wide = jnp.where(spread_col == 3 * spread_row + field, 1.0, 0.0).astype(BF16)
            mix_in.append(jnp.dot(into_parts[part], wide, preferred_element_type=F32))
            tall = jnp.where(tall_row == 3 * tall_col + field, 1.0, 0.0).astype(BF16)
            mix_out.append(jnp.dot(tall, out_parts[part], preferred_element_type=F32))
    mix_in = jnp.concatenate(mix_in, axis=0).astype(BF16)
    mix_high = jnp.concatenate(mix_out[:2] + mix_out[:2], axis=1).astype(BF16)
    mix_low = jnp.concatenate(mix_out[2:], axis=1).astype(BF16)
    diffusion = jnp.sum(
        jnp.where(tall_row == 3 * tall_col, hyper_ref[...], 0.0), axis=1, keepdims=True
    )
    is_vorticity = lax.broadcasted_iota(jnp.int32, (cols, 256), 0) % 3 == 0

    for group in range(owners // 4):
        parts = [q_ref[(group * 4 + i) * cols : (group * 4 + i + 1) * cols, :] for i in range(4)]
        turned = swap_blocks(parts)
        for i in range(4):
            part = i % 2
            grid_ref[i // 2, part * cols : (part + 1) * cols, group * 128 : (group + 1) * 128] = (
                turned[i]
            )

    nt = (((1,), (1,)), ((), ()))
    for pair in range(rows // 256):
        here = slice(pair * 256, (pair + 1) * 256)
        slot = (2 * pair >= count0).astype(jnp.int32)
        found = lax.dot_general(
            grid_ref[slot], legendre_ref[here, :], nt, preferred_element_type=F32
        )
        spec_ref[:, here] = (found * usable_f[:1, here]).astype(BF16)

    @pl.when(straddles)
    def _():
        found = lax.dot_general(
            grid_ref[1], legendre_ref[pl.ds(cut, BLK), :], nt, preferred_element_type=F32
        )
        at = lax.broadcasted_iota(jnp.int32, (8, BLK), 1) + cut
        _, _, keep = layout_at(at, waves, window)
        keep = jnp.where(keep, 1.0, 0.0)
        spec_ref[:, pl.ds(cut, BLK)] = (found * keep[:1]).astype(BF16)

    for part in range(2):
        for pair in range(rows // 256):
            here = slice(pair * 256, (pair + 1) * 256)
            modes = jnp.dot(
                mix_in,
                spec_ref[part * cols : (part + 1) * cols, here],
                preferred_element_type=F32,
            )
            div = modes[:levels] + modes[2 * levels : 3 * levels]
            temp = modes[levels : 2 * levels] + modes[3 * levels :]
            right_ref[part, :, here] = (div - wave_factor[:1, here] * temp) * inverse[:, here]
            temp_ref[part, :, here] = temp

    for part in range(2):
        for start in range(0, levels, 8):
            mine = slice(start, start + 8)
            right = right_ref[part, mine, :]
            answer = right
            for _ in range(SWEEPS - 1):
                around = links_ref[0] * pltpu.roll(answer, 2, 1)
                around = around + links_ref[1] * pltpu.roll(answer, 1, 1)
                around = around + links_ref[2] * pltpu.roll(answer, rows - 1, 1)
                around = around + links_ref[3] * pltpu.roll(answer, rows - 2, 1)
                answer = right - scale_ref[mine, :] * around
            right_ref[part, mine, :] = answer

    for pair in range(rows // 256):
        here = slice(pair * 256, (pair + 1) * 256)
        factor = wave_factor[:1, here]
        damped = usable_f[:1, here] / (1.0 + diffusion * factor * factor)
        for part in range(2):
            answer = right_ref[part, :, here]
            temp = temp_ref[part, :, here] - 0.5 * answer
            high, low = split(jnp.concatenate([answer, temp], axis=0))
            mixed = jnp.dot(
                mix_high, jnp.concatenate([high, low], axis=0), preferred_element_type=F32
            ) + jnp.dot(mix_low, high, preferred_element_type=F32)
            vorticity = spec_ref[part * cols : (part + 1) * cols, here].astype(F32) * damped
            mixed = jnp.where(is_vorticity, vorticity, mixed * usable_f[:1, here])
            update_ref[part * cols : (part + 1) * cols, here] = mixed.astype(BF16)

    total_ref[...] = jnp.zeros_like(total_ref)
    for pair in range(rows // 256):
        here = slice(pair * 256, (pair + 1) * 256)
        slot = (2 * pair >= count0).astype(jnp.int32)
        values = update_ref[:, here]
        spills = jnp.logical_and(straddles, count0 == 2 * pair + 1)
        lane = lax.broadcasted_iota(jnp.int32, values.shape, 1)
        values = jnp.where(jnp.logical_and(spills, lane >= BLK), jnp.zeros_like(values), values)
        total_ref[slot] += jnp.dot(values, legendre_ref[here, :], preferred_element_type=F32)

    @pl.when(straddles)
    def _():
        total_ref[1] += jnp.dot(
            update_ref[:, pl.ds(cut, BLK)],
            legendre_ref[pl.ds(cut, BLK), :],
            preferred_element_type=F32,
        )

    for group in range(owners // 4):
        parts = [
            total_ref[
                i // 2, (i % 2) * cols : (i % 2 + 1) * cols, group * 128 : (group + 1) * 128
            ].astype(BF16)
            for i in range(4)
        ]
        turned = swap_blocks(parts)
        for i in range(4):
            out_ref[(group * 4 + i) * cols : (group * 4 + i + 1) * cols, :] = turned[i]


VMEM = pl.BlockSpec(memory_space=pltpu.VMEM)
SMEM = pl.BlockSpec(memory_space=pltpu.SMEM)


def exchange(rows):
    devices = lax.axis_size("lat") * lax.axis_size("mode")
    chunks = rows.reshape(devices, rows.shape[0] // (2 * devices), 2, rows.shape[1])
    return lax.all_to_all(chunks, ("lat", "mode"), 0, 0, tiled=True).reshape(rows.shape)


def body(
    fourier,
    wave_table,
    legendre,
    coupling,
    gravity,
    hyper_diff,
    strata_into_eigenbasis,
    vertical_out,
):
    window = fourier.shape[4] // 2
    owners = wave_table.shape[0]
    levels = gravity.shape[0]
    size = fourier.size // LANES
    rows = legendre.shape[1] * legendre.shape[2]
    latitudes = legendre.shape[3]
    flat = jax.ShapeDtypeStruct((size, LANES), BF16)
    limit = pltpu.CompilerParams(vmem_limit_bytes=56 * 1024 * 1024)
    sending = pl.pallas_call(
        functools.partial(pack_kernel, owners=owners, window=window),
        out_shape=flat,
        in_specs=[VMEM, VMEM],
        out_specs=VMEM,
        scratch_shapes=[pltpu.VMEM((size, LANES), F32)],
        compiler_params=limit,
        name="pack",
    )(wave_table, fourier.reshape(size, LANES))
    at_owner = exchange(sending)
    me = lax.axis_index("lat").astype(jnp.int32).reshape(1)
    synthesis = pl.pallas_call(
        functools.partial(owner_kernel, window=window, levels=levels),
        out_shape=flat,
        in_specs=[SMEM, SMEM] + [VMEM] * 7,
        out_specs=VMEM,
        scratch_shapes=[
            pltpu.VMEM((2, 6 * levels, latitudes), BF16),
            pltpu.VMEM((6 * levels, rows), BF16),
            pltpu.VMEM((2, levels, rows), F32),
            pltpu.VMEM((2, levels, rows), F32),
            pltpu.VMEM((levels, rows), F32),
            pltpu.VMEM((4, 8, rows), F32),
            pltpu.VMEM((6 * levels, rows), BF16),
            pltpu.VMEM((2, 6 * levels, latitudes), F32),
        ],
        compiler_params=limit,
        name="owner",
    )(
        me,
        wave_table,
        at_owner,
        legendre.reshape(rows, latitudes),
        coupling.reshape(coupling.shape[0], rows),
        gravity.reshape(1, levels),
        hyper_diff.reshape(1, levels),
        strata_into_eigenbasis,
        vertical_out,
    )
    returned = exchange(synthesis)
    result = pl.pallas_call(
        functools.partial(unpack_kernel, owners=owners, window=window),
        out_shape=flat,
        in_specs=[VMEM, VMEM],
        out_specs=VMEM,
        scratch_shapes=[pltpu.VMEM((size, LANES), F32)],
        compiler_params=limit,
        name="unpack",
    )(wave_table, returned)
    return result.reshape(fourier.shape)


def solution(mesh):
    placed = (
        P(None, "mode", None, "lat", None),
        P(),
        P("lat", None, None, None),
        P(None, "lat", None),
        P(),
        P(),
        P(),
        P(),
    )
    return jax.shard_map(
        body,
        mesh=mesh,
        in_specs=placed,
        out_specs=P(None, "mode", None, "lat", None),
        check_vma=False,
    )
```

time: 390 us -> 115 us (0.29)
  local copies, waits for them, and re-layouts: 144 us -> 2.99 us
  loops' own time: 62.1 us -> 0 us
  matrix products: 44.5 us -> 0 us
  other arithmetic: 28.9 us -> 0 us
  Pallas kernels: 0 us -> 22 us
  starting transfers between devices: 28.8 us -> 15.7 us
  waiting for transfers between devices: 42.7 us -> 33.2 us
  blocking collectives: 35 us -> 41 us
    another operation x2 -> x0, loops' own time: 62.1 us -> none  [the longest x1 31.5 us: to_spectral(): lax.fori_loop(0, tables.shape[0], to_one_block, jnp.zeros((flat.shape[1],...]
    dot_general x36 -> x0, matrix products: 44.5 us -> none  [the longest x16 20.9 us: to_one_block(): jnp.einsum('nl,cl->cn', table, picked, preferred_element_type=jnp.float32)]
    all_to_all x7 -> x0, local copies, waits for them, and re-layouts: 41.8 us -> none  [the longest x3 20 us: body(): lax.all_to_all(synthesis.reshape(at_owner.shape), 'lat', split_axis=5, co...]
    unnamed x23 -> x6, local copies, waits for them, and re-layouts: 28.2 us -> 2.99 us
    reshape x7 -> x0, local copies, waits for them, and re-layouts: 23.8 us -> none  [the longest x2 12.2 us: body(): split_parts = fourier.reshape(fourier.shape[:4] + (2, window))]
    pallas_call x0 -> x3, Pallas kernels: none -> 22 us  [the longest x1 10.9 us: body(): pl.pallas_call(functools.partial(owner_kernel, window=window, levels=leve...]
    dynamic_slice x48 -> x0, local copies, waits for them, and re-layouts: 21.8 us -> none  [the longest x16 10.4 us: synthesise_one_block(): slot = member_block[index]]
    all_to_all x3 -> x1, starting transfers between devices: 28.8 us -> 15.7 us  [exchange(): lax.all_to_all(chunks, ('lat', 'mode'), 0, 0, tiled=True)]
  transfers between devices with their start and end apart: 3 -> 1, of which waited for: 3 -> 1; matrix products, arithmetic and copies ran while one was open for 5% -> 1% of each run, Pallas kernels for 0% -> 0%
where the time goes in v1:
time: 115 us
  blocking collectives  41 us (36%)
  waiting for transfers between devices  33.2 us (29%)
  Pallas kernels  22 us (19%)
  starting transfers between devices  15.7 us (14%)
  local copies, waits for them, and re-layouts  2.99 us (3%)
    all_to_all x1, blocking collectives, exchange(): lax.all_to_all(chunks, ('lat', 'mode'), 0, 0, tiled=True)  41 us
    all_to_all x1, waiting for transfers between devices, exchange(): lax.all_to_all(chunks, ('lat', 'mode'), 0, 0, tiled=True)  33.2 us
    all_to_all x1, starting transfers between devices, exchange(): lax.all_to_all(chunks, ('lat', 'mode'), 0, 0, tiled=True)  15.7 us
    pallas_call x1, Pallas kernels, body(): pl.pallas_call(functools.partial(owner_kernel, window=window, levels=leve...  10.9 us
    pallas_call x1, Pallas kernels, body(): pl.pallas_call(functools.partial(pack_kernel, owners=owners, window=windo...  5.61 us
    pallas_call x1, Pallas kernels, body(): pl.pallas_call(functools.partial(unpack_kernel, owners=owners, window=win...  5.46 us
    unnamed x6, local copies, waits for them, and re-layouts  2.99 us
  transfers between devices with their start and end apart: 1, of which 1 were waited for; matrix products, arithmetic and copies ran while one was open for 1% of the time, Pallas kernels for 0%

profile of v1, /device:TPU:1, one launch (start us, length us, event | category | flops | bytes accessed | tf_op | source)
XLA Modules:
  0.0 114.8 jit_solution(8016221098957262589)
XLA Ops:
  0.0 1.4 %copy.11.table_ref = s32[32,2]{1,0:T(8,128)} copy(s32[32,2]{0,1:T(2,128)} %param.9) | data formatting | bytes 512 | tf_op args[1]
  1.4 5.6 %pack.1 = bf16[4608,128]{1,0:T(8,128)(2,1)} custom-call(s32[32,2]{1,0:T(8,128)} %copy.11.table_ref, bf16[4608,128]{1,0:T(8,128)(2,1)} %bitcast.18), custom_call_target="tpu_custom_call" | custom-call | tf_op jit(solution)/shard_map/pack/pallas_call | solution.py:294
  7.0 0.0 copy-start.1
  7.0 15.7 %all-to-all-start = ((bf16[256,9,2,128]{3,2,1,0:T(2,128)(2,1)}), bf16[256,9,2,128]{3,2,1,0:T(2,128)(2,1)S(1)}, u32[]{:S(2)}, u32[]{:S(2)}) async-start(bf16[256,9,2,128]{3,2,1,0:T(2,128)(2,1)} %bitcast.13), calls=%async_computation | async-start | bytes 2359296 | tf_op jit(solution)/shard_map/all_to_all | solution.py:273
  22.6 0.0 copy-done.1
  22.6 0.6 copy.14
  23.3 33.2 %all-to-all-done = bf16[256,9,2,128]{3,2,1,0:T(2,128)(2,1)S(1)} async-done(((bf16[256,9,2,128]{3,2,1,0:T(2,128)(2,1)}), bf16[256,9,2,128]{3,2,1,0:T(2,128)(2,1)S(1)}, u32[]{:S(2)}, u32[]{:S(2)}) %all-to-all-start) | async-done | bytes 1179680 | tf_op jit(solution)/shard_map/all_to_all | solution.py:273
  56.4 0.0 copy-start
  56.4 1.0 copy-done
  57.5 10.9 %owner.1 = bf16[4608,128]{1,0:T(8,128)(2,1)} custom-call(s32[1]{0:T(128)} %bitcast.me_ref, s32[32,2]{1,0:T(8,128)} %copy.11.table_ref, bf16[4608,128]{1,0:T(8,128)(2,1)} %bitcast.15, bf16[2048,1024]{1,0:T(8,128)(2,1)} %bitcast.17, f32[4,2048]{1,0:T(4,128)} %bitcast.19, f32[1,48]{1,0:T(1,128)} %bitcast.20, f32[1,48]{1,0:T(1,128)} %bitcast.21, ...), custom_call_target="tpu_custom_call" | custom-call | tf_op jit(solution)/shard_map/owner/pallas_call | solution.py:305
  68.3 41.0 %all_to_all.10 = bf16[256,9,2,128]{3,2,1,0:T(2,128)(2,1)} all-to-all(bf16[256,9,2,128]{3,2,1,0:T(2,128)(2,1)} %bitcast.16), channel_id=1, replica_groups=mesh['lat'=32,'mode'=8] {'lat','mode'}, dimensions={0} | all-to-all | bytes 2359296 | tf_op jit(solution)/shard_map/all_to_all | solution.py:273
  109.3 5.5 %unpack.1 = bf16[4608,128]{1,0:T(8,128)(2,1)} custom-call(s32[32,2]{1,0:T(8,128)} %copy.11.table_ref, bf16[4608,128]{1,0:T(8,128)(2,1)} %bitcast.14), custom_call_target="tpu_custom_call" | custom-call | tf_op jit(solution)/shard_map/unpack/pallas_call | solution.py:334
Async XLA Ops:
  7.0 15.7 %copy-start.1 = (f32[4,1,2048]{2,1,0:T(1,128)S(1)}, f32[4,1,2048]{2,1,0:T(1,128)}, u32[]{:S(2)}) copy-start(f32[4,1,2048]{2,1,0:T(1,128)} %param.11) | copy-start | bytes 98308
  7.0 49.5 %all-to-all-start = ((bf16[256,9,2,128]{3,2,1,0:T(2,128)(2,1)}), bf16[256,9,2,128]{3,2,1,0:T(2,128)(2,1)S(1)}, u32[]{:S(2)}, u32[]{:S(2)}) async-start(bf16[256,9,2,128]{3,2,1,0:T(2,128)(2,1)} %bitcast.13), calls=%async_computation | async-start | bytes 2359296 | tf_op jit(solution)/shard_map/all_to_all | solution.py:273
  56.4 1.0 copy-start

commit v2 on v1

v2 whole, which is shorter than its diff:
```python
import functools

import jax
import jax.numpy as jnp
from jax import lax
from jax.experimental import pallas as pl
from jax.experimental.pallas import tpu as pltpu
from jax.sharding import PartitionSpec as P

NN = 1792
BLK = 128
SWEEPS = 3
LANES = 128
BAND = 32
F32 = jnp.float32
BF16 = jnp.bfloat16


def swap_blocks(parts):
    y0, y1, y2, y3 = parts
    lane = lax.broadcasted_iota(jnp.int32, y0.shape, 1)
    low = lane < 64
    n0 = jnp.where(low, y0, pltpu.roll(y2, 64, 1))
    n2 = jnp.where(low, pltpu.roll(y0, 64, 1), y2)
    n1 = jnp.where(low, y1, pltpu.roll(y3, 64, 1))
    n3 = jnp.where(low, pltpu.roll(y1, 64, 1), y3)
    even = (lane & 32) == 0
    z0 = jnp.where(even, n0, pltpu.roll(n1, 32, 1))
    z1 = jnp.where(even, pltpu.roll(n0, 96, 1), n1)
    z2 = jnp.where(even, n2, pltpu.roll(n3, 32, 1))
    z3 = jnp.where(even, pltpu.roll(n2, 96, 1), n3)
    return z0, z1, z2, z3


def wave_selector(table_ref, owners, window):
    lane = lax.broadcasted_iota(jnp.int32, (owners, LANES), 1).astype(F32)
    rows = []
    for slot in range(2):
        waves = column_of(table_ref[slot : slot + 1, :].astype(F32), owners)
        for part in range(2):
            rows.append(jnp.where(waves + part * window == lane, 1.0, 0.0))
    return jnp.concatenate(rows, axis=0).astype(BF16)


def pack_kernel(
    table_ref, x_ref, out_ref, table, held, stage_ref, load_sem, table_sem, *, owners, window
):
    columns = x_ref.shape[0] // BAND
    loads = load_sem.shape[0]
    part_rows = x_ref.shape[0] // loads
    fetch = pltpu.make_async_copy(table_ref, table, table_sem)
    fetch.start()
    copies = []
    for i in range(loads):
        here = pl.ds(i * part_rows, part_rows)
        copies.append(pltpu.make_async_copy(x_ref.at[here], held.at[here], load_sem.at[i]))
        copies[i].start()
    fetch.wait()
    selector = wave_selector(table, owners, window)
    ready = 0
    for pair in range(columns // 8):
        while ready * part_rows < (pair + 1) * 256:
            copies[ready].wait()
            ready += 1
        both = lax.dot_general(
            selector,
            held[pair * 256 : (pair + 1) * 256, :],
            (((1,), (1,)), ((), ())),
            preferred_element_type=F32,
        ).astype(BF16)
        for half in range(2):
            turned = both[:, half * 128 : (half + 1) * 128]
            parts = swap_blocks([turned[i * owners : (i + 1) * owners] for i in range(4)])
            for i in range(4):
                here = pl.ds(pair * 8 + half * 4 + i, owners, stride=columns + 1)
                stage_ref[here, :] = parts[i].astype(F32)
    for owner in range(owners):
        start = owner * (columns + 1)
        out_ref[owner * columns : (owner + 1) * columns, :] = stage_ref[
            start : start + columns, :
        ].astype(BF16)


def unpack_kernel(
    table_ref, x_ref, out_ref, held, stage_ref, store_sem, *, owners, window
):
    selector = wave_selector(table_ref, owners, window)
    columns = out_ref.shape[0] // BAND
    stores = store_sem.shape[0]
    part_rows = out_ref.shape[0] // stores
    for owner in range(owners):
        start = owner * (columns + 1)
        stage_ref[start : start + columns, :] = x_ref[
            owner * columns : (owner + 1) * columns, :
        ].astype(F32)
    square = (LANES, LANES)
    same = lax.broadcasted_iota(jnp.int32, square, 0) == lax.broadcasted_iota(jnp.int32, square, 1)
    identity = jnp.where(same, 1.0, 0.0).astype(BF16)
    copies = []
    for i in range(stores):
        here = pl.ds(i * part_rows, part_rows)
        copies.append(pltpu.make_async_copy(held.at[here], out_ref.at[here], store_sem.at[i]))
    sent = 0
    for first in range(0, columns // 4, 4):
        upright = []
        for group in range(first, first + 4):
            parts = [
                stage_ref[pl.ds(group * 4 + i, owners, stride=columns + 1), :].astype(BF16)
                for i in range(4)
            ]
            turned = jnp.concatenate(swap_blocks(parts), axis=0)
            upright.append(
                lax.dot_general(
                    identity, turned, (((1,), (1,)), ((), ())), preferred_element_type=F32
                )
            )
        upright = jnp.concatenate(upright, axis=0).astype(BF16)
        rows = jnp.dot(upright, selector, preferred_element_type=F32)
        held[first * 128 : (first + 4) * 128, :] = rows.astype(BF16)
        while sent < stores and (sent + 1) * part_rows <= (first + 4) * 128:
            copies[sent].start()
            sent += 1
    for copy in copies:
        copy.wait()


def layout_at(index, waves, window):
    blocks = NN // BLK
    low0, low1 = (waves[0] * NN) // window, (waves[1] * NN) // window
    first0, first1 = low0 // BLK, low1 // BLK
    count0, count1 = blocks - first0, blocks - first1
    block = index >> 7
    lead = block < count0
    held = jnp.logical_and(index >= 0, block < count0 + count1)
    degree = jnp.where(lead, first0 * BLK, (first1 - count0) * BLK) + index
    usable = jnp.logical_and(held, degree >= jnp.where(lead, low0, low1))
    return lead, jnp.where(usable, degree, 0), usable


def split(values):
    high = values.astype(BF16)
    return high, (values - high.astype(F32)).astype(BF16)


def column_of(row, size):
    diagonal = lax.broadcasted_iota(jnp.int32, (size, size), 0) == lax.broadcasted_iota(
        jnp.int32, (size, size), 1
    )
    return jnp.sum(jnp.where(diagonal, row, 0.0), axis=1, keepdims=True)


def setup_kernel(
    me_ref,
    table_ref,
    coupling_ref,
    gravity_ref,
    hyper_ref,
    into_ref,
    out_of_ref,
    links_ref,
    scale_ref,
    inverse_ref,
    damped_ref,
    lines_ref,
    mix_in_ref,
    mix_out_ref,
    mix_low_ref,
    *,
    window,
):
    rows = coupling_ref.shape[2]
    levels = gravity_ref.shape[1]
    cols = 3 * levels
    waves = (table_ref[0, me_ref[0]], table_ref[1, me_ref[0]])
    index = lax.broadcasted_iota(jnp.int32, (8, rows), 1)
    lead, degree, usable = layout_at(index, waves, window)
    wave_factor = (degree * (degree + 1)).astype(F32) / float(NN * NN)
    usable_f = jnp.where(usable, 1.0, 0.0)
    lines_ref[0:1, :] = wave_factor[:1]
    lines_ref[1:2, :] = usable_f[:1]
    for number, distance in enumerate((-2, -1, 1, 2)):
        other_lead, _, other_usable = layout_at(index + distance, waves, window)
        joined = jnp.logical_and(jnp.logical_and(usable, other_usable), lead == other_lead)
        inside = jnp.logical_and(index + distance >= 0, index + distance < rows)
        joined = jnp.logical_and(joined, inside)
        links_ref[number : number + 1, :] = jnp.where(joined[:1], coupling_ref[number], 0.0)
    gravity = column_of(gravity_ref[...], levels)
    hyper = column_of(hyper_ref[...], levels)
    weighted = gravity * wave_factor[:1]
    inverse = usable_f[:1] / (1.0 + weighted)
    scale_ref[...] = weighted * inverse
    inverse_ref[...] = inverse
    damped_ref[...] = usable_f[:1] / (1.0 + hyper * (wave_factor[:1] * wave_factor[:1]))

    wide_row = lax.broadcasted_iota(jnp.int32, (levels, cols), 0)
    wide_col = lax.broadcasted_iota(jnp.int32, (levels, cols), 1)
    tall_row = lax.broadcasted_iota(jnp.int32, (cols, levels), 0)
    tall_col = lax.broadcasted_iota(jnp.int32, (cols, levels), 1)
    wide, tall = [], []
    for field in range(3):
        wide.append(jnp.where(wide_col == 3 * wide_row + field, 1.0, 0.0).astype(BF16))
        tall.append(jnp.where(tall_row == 3 * tall_col + field, 1.0, 0.0).astype(BF16))
    into_parts = split(into_ref[...])
    out_parts = split(out_of_ref[...])
    mix_in, mix_out = [wide[0].astype(F32)], []
    for part in range(2):
        for field in (1, 2):
            mix_in.append(jnp.dot(into_parts[part], wide[field], preferred_element_type=F32))
            mix_out.append(jnp.dot(tall[field], out_parts[part], preferred_element_type=F32))
    mix_in_ref[...] = jnp.concatenate(mix_in, axis=0).astype(BF16)
    mix_out_ref[...] = jnp.concatenate(
        [tall[0].astype(F32)] + mix_out[:2] + mix_out[:2], axis=1
    ).astype(BF16)
    mix_low_ref[...] = jnp.concatenate(mix_out[2:], axis=1).astype(BF16)


def owner_kernel(
    me_ref,
    table_ref,
    q_ref,
    source_ref,
    links_ref,
    scale_ref,
    inverse_ref,
    damped_ref,
    lines_ref,
    mix_in_ref,
    mix_out_ref,
    mix_low_ref,
    out_ref,
    grid_ref,
    spec_ref,
    right_ref,
    temp_ref,
    vort_ref,
    update_ref,
    total_ref,
    legendre_ref,
    load_sem,
    *,
    window,
):
    levels, rows = scale_ref.shape
    pairs = rows // 256
    loads = []
    for pair in range(pairs):
        here = pl.ds(pair * 256, 256)
        loads.append(
            pltpu.make_async_copy(source_ref.at[here], legendre_ref.at[here], load_sem.at[pair])
        )
        loads[pair].start()
    cols = 3 * levels
    owners = q_ref.shape[0] // cols
    count0 = NN // BLK - (table_ref[0, me_ref[0]] * NN) // window // BLK
    straddles = count0 % 2 == 1
    cut = pl.multiple_of(count0 * BLK, BLK)

    for group in range(owners // 4):
        parts = [q_ref[(group * 4 + i) * cols : (group * 4 + i + 1) * cols, :] for i in range(4)]
        turned = swap_blocks(parts)
        for i in range(4):
            part = i % 2
            grid_ref[i // 2, part * cols : (part + 1) * cols, group * 128 : (group + 1) * 128] = (
                turned[i]
            )

    nt = (((1,), (1,)), ((), ()))
    for pair in range(pairs):
        here = slice(pair * 256, (pair + 1) * 256)
        slot = (2 * pair >= count0).astype(jnp.int32)
        if pair in (0, 4):
            for load in loads[pair : pair + 4]:
                load.wait()
        found = lax.dot_general(
            grid_ref[slot], legendre_ref[here, :], nt, preferred_element_type=F32
        )
        spec_ref[:, here] = (found * lines_ref[1:2, here]).astype(BF16)

    @pl.when(straddles)
    def _():
        found = lax.dot_general(
            grid_ref[1], legendre_ref[pl.ds(cut, BLK), :], nt, preferred_element_type=F32
        )
        spec_ref[:, pl.ds(cut, BLK)] = (found * lines_ref[1:2, pl.ds(cut, BLK)]).astype(BF16)

    for part in range(2):
        for pair in range(pairs):
            here = slice(pair * 256, (pair + 1) * 256)
            modes = jnp.dot(
                mix_in_ref[...],
                spec_ref[part * cols : (part + 1) * cols, here],
                preferred_element_type=F32,
            )
            vort_ref[part, :, here] = (modes[:levels] * damped_ref[:, here]).astype(BF16)
            div = modes[levels : 2 * levels] + modes[3 * levels : 4 * levels]
            temp = modes[2 * levels : 3 * levels] + modes[4 * levels :]
            right_ref[part, :, here] = (div - lines_ref[0:1, here] * temp) * inverse_ref[:, here]
            temp_ref[part, :, here] = temp

    for part in range(2):
        for start in range(0, levels, 8):
            mine = slice(start, start + 8)
            right = right_ref[part, mine, :]
            answer = right
            for _ in range(SWEEPS - 1):
                around = links_ref[0 : 1, :] * pltpu.roll(answer, 2, 1)
                around = around + links_ref[1 : 2, :] * pltpu.roll(answer, 1, 1)
                around = around + links_ref[2 : 3, :] * pltpu.roll(answer, rows - 1, 1)
                around = around + links_ref[3 : 4, :] * pltpu.roll(answer, rows - 2, 1)
                answer = right - scale_ref[mine, :] * around
            right_ref[part, mine, :] = answer

    for pair in range(pairs):
        here = slice(pair * 256, (pair + 1) * 256)
        for part in range(2):
            answer = right_ref[part, :, here]
            temp = temp_ref[part, :, here] - 0.5 * answer
            high, low = split(jnp.concatenate([answer, temp], axis=0))
            mixed = jnp.dot(
                mix_out_ref[...],
                jnp.concatenate([vort_ref[part, :, here], high, low], axis=0),
                preferred_element_type=F32,
            ) + jnp.dot(mix_low_ref[...], high, preferred_element_type=F32)
            update_ref[part * cols : (part + 1) * cols, here] = mixed.astype(BF16)

    for pair in (0, pairs - 1) + tuple(range(1, pairs - 1)):
        here = slice(pair * 256, (pair + 1) * 256)
        slot = (2 * pair >= count0).astype(jnp.int32)
        values = update_ref[:, here]
        spills = count0 == 2 * pair + 1
        lane = lax.broadcasted_iota(jnp.int32, values.shape, 1)
        values = jnp.where(jnp.logical_and(spills, lane >= BLK), jnp.zeros_like(values), values)
        term = jnp.dot(values, legendre_ref[here, :], preferred_element_type=F32)
        if pair == 0:
            total_ref[0] = term
        elif pair == pairs - 1:
            total_ref[1] = term
        else:
            total_ref[slot] += term

    @pl.when(straddles)
    def _():
        total_ref[1] += jnp.dot(
            update_ref[:, pl.ds(cut, BLK)],
            legendre_ref[pl.ds(cut, BLK), :],
            preferred_element_type=F32,
        )

    for group in range(owners // 4):
        parts = [
            total_ref[
                i // 2, (i % 2) * cols : (i % 2 + 1) * cols, group * 128 : (group + 1) * 128
            ].astype(BF16)
            for i in range(4)
        ]
        turned = swap_blocks(parts)
        for i in range(4):
            out_ref[(group * 4 + i) * cols : (group * 4 + i + 1) * cols, :] = turned[i]


VMEM = pl.BlockSpec(memory_space=pltpu.VMEM)
SMEM = pl.BlockSpec(memory_space=pltpu.SMEM)
HBM = pl.BlockSpec(memory_space=pltpu.HBM)
MIB = 1024 * 1024


def exchange(rows):
    devices = lax.axis_size("lat") * lax.axis_size("mode")
    chunks = rows.reshape(devices, rows.shape[0] // (2 * devices), 2, rows.shape[1])
    return lax.all_to_all(chunks, ("lat", "mode"), 0, 0, tiled=True).reshape(rows.shape)


def body(
    fourier,
    wave_table,
    legendre,
    coupling,
    gravity,
    hyper_diff,
    strata_into_eigenbasis,
    vertical_out,
):
    window = fourier.shape[4] // 2
    owners = wave_table.shape[0]
    levels = gravity.shape[0]
    size = fourier.size // LANES
    table = wave_table.T
    rows = legendre.shape[1] * legendre.shape[2]
    latitudes = legendre.shape[3]
    flat = jax.ShapeDtypeStruct((size, LANES), BF16)
    cols = 3 * levels
    staged = owners * (size // BAND + 1)
    sending = pl.pallas_call(
        functools.partial(pack_kernel, owners=owners, window=window),
        out_shape=flat,
        in_specs=[HBM, HBM],
        out_specs=VMEM,
        scratch_shapes=[
            pltpu.VMEM((2, owners), jnp.int32),
            pltpu.VMEM((size, LANES), BF16),
            pltpu.VMEM((staged, LANES), F32),
            pltpu.SemaphoreType.DMA((4,)),
            pltpu.SemaphoreType.DMA,
        ],
        compiler_params=pltpu.CompilerParams(vmem_limit_bytes=60 * MIB),
        name="pack",
    )(table, fourier.reshape(size, LANES))
    at_owner = exchange(sending)
    me = lax.axis_index("lat").astype(jnp.int32).reshape(1)
    prepared = pl.pallas_call(
        functools.partial(setup_kernel, window=window),
        out_shape=[
            jax.ShapeDtypeStruct((4, rows), F32),
            jax.ShapeDtypeStruct((levels, rows), F32),
            jax.ShapeDtypeStruct((levels, rows), F32),
            jax.ShapeDtypeStruct((levels, rows), F32),
            jax.ShapeDtypeStruct((2, rows), F32),
            jax.ShapeDtypeStruct((5 * levels, cols), BF16),
            jax.ShapeDtypeStruct((cols, 5 * levels), BF16),
            jax.ShapeDtypeStruct((cols, 2 * levels), BF16),
        ],
        in_specs=[SMEM, SMEM] + [VMEM] * 5,
        out_specs=[VMEM] * 8,
        compiler_params=pltpu.CompilerParams(vmem_limit_bytes=16 * MIB),
        name="setup",
    )(
        me,
        table,
        coupling,
        gravity.reshape(1, levels),
        hyper_diff.reshape(1, levels),
        strata_into_eigenbasis,
        vertical_out,
    )
    synthesis = pl.pallas_call(
        functools.partial(owner_kernel, window=window),
        out_shape=flat,
        in_specs=[SMEM, SMEM, VMEM, HBM] + [VMEM] * 8,
        out_specs=VMEM,
        scratch_shapes=[
            pltpu.VMEM((2, 2 * cols, latitudes), BF16),
            pltpu.VMEM((2 * cols, rows), BF16),
            pltpu.VMEM((2, levels, rows), F32),
            pltpu.VMEM((2, levels, rows), F32),
            pltpu.VMEM((2, levels, rows), BF16),
            pltpu.VMEM((2 * cols, rows), BF16),
            pltpu.VMEM((2, 2 * cols, latitudes), F32),
            pltpu.VMEM((rows, latitudes), BF16),
            pltpu.SemaphoreType.DMA((rows // 256,)),
        ],
        input_output_aliases={2: 0},
        compiler_params=pltpu.CompilerParams(vmem_limit_bytes=48 * MIB),
        name="owner",
    )(me, table, at_owner, legendre.reshape(rows, latitudes), *prepared)
    returned = exchange(synthesis)
    result = pl.pallas_call(
        functools.partial(unpack_kernel, owners=owners, window=window),
        out_shape=flat,
        in_specs=[VMEM, VMEM],
        out_specs=HBM,
        scratch_shapes=[
            pltpu.VMEM((size, LANES), BF16),
            pltpu.VMEM((staged, LANES), F32),
            pltpu.SemaphoreType.DMA((8,)),
        ],
        compiler_params=pltpu.CompilerParams(vmem_limit_bytes=8 * MIB),
        name="unpack",
    )(table, returned)
    return result.reshape(fourier.shape)


def solution(mesh):
    placed = (
        P(None, "mode", None, "lat", None),
        P(),
        P("lat", None, None, None),
        P(None, "lat", None),
        P(),
        P(),
        P(),
        P(),
    )
    return jax.shard_map(
        body,
        mesh=mesh,
        in_specs=placed,
        out_specs=P(None, "mode", None, "lat", None),
        check_vma=False,
    )
```

time: 115 us -> 106 us (0.922)
  Pallas kernels: 22 us -> 17.8 us
  local copies, waits for them, and re-layouts: 2.99 us -> 0.04 us
  blocking collectives: 41 us -> 39.6 us
    unnamed x6 -> x12, local copies, waits for them, and re-layouts: 2.99 us -> 0.04 us
    pallas_call x1, Pallas kernels: 5.46 us -> 2.89 us  [body(): pl.pallas_call(functools.partial(unpack_kernel, owners=owners, window=win...]
    pallas_call x1, Pallas kernels: 5.61 us -> 3.75 us  [body(): pl.pallas_call(functools.partial(pack_kernel, owners=owners, window=windo...]
    all_to_all x1, blocking collectives: 41 us -> 39.6 us  [exchange(): lax.all_to_all(chunks, ('lat', 'mode'), 0, 0, tiled=True)]
    pallas_call x1 -> x2, Pallas kernels: 10.9 us -> 11.2 us  [the longest x1 9.97 us: body(): pl.pallas_call(functools.partial(owner_kernel, window=window), out_shape=...]
  transfers between devices with their start and end apart: 1 -> 1, of which waited for: 1 -> 1; matrix products, arithmetic and copies ran while one was open for 1% -> 0% of each run, Pallas kernels for 0% -> 1%
where the time goes in v2:
time: 106 us
  blocking collectives  39.6 us (37%)
  waiting for transfers between devices  32.5 us (31%)
  Pallas kernels  17.8 us (17%)
  starting transfers between devices  15.7 us (15%)
    all_to_all x1, blocking collectives, exchange(): lax.all_to_all(chunks, ('lat', 'mode'), 0, 0, tiled=True)  39.6 us
    all_to_all x1, waiting for transfers between devices, exchange(): lax.all_to_all(chunks, ('lat', 'mode'), 0, 0, tiled=True)  32.5 us
    all_to_all x1, starting transfers between devices, exchange(): lax.all_to_all(chunks, ('lat', 'mode'), 0, 0, tiled=True)  15.7 us
    pallas_call x1, Pallas kernels, body(): pl.pallas_call(functools.partial(owner_kernel, window=window), out_shape=...  9.97 us
    pallas_call x1, Pallas kernels, body(): pl.pallas_call(functools.partial(pack_kernel, owners=owners, window=windo...  3.75 us
    pallas_call x1, Pallas kernels, body(): pl.pallas_call(functools.partial(unpack_kernel, owners=owners, window=win...  2.89 us
  transfers between devices with their start and end apart: 1, of which 1 were waited for; matrix products, arithmetic and copies ran while one was open for 0% of the time, Pallas kernels for 1%

profile of v2, /device:TPU:1, one launch (start us, length us, event | category | flops | bytes accessed | tf_op | source)
XLA Modules:
  0.0 105.8 jit_solution(5181605171594871769)
XLA Ops:
  0.0 3.8 %pack.1 = bf16[4608,128]{1,0:T(8,128)(2,1)} custom-call(s32[2,32]{1,0:T(2,128)} %bitcast.14, bf16[4608,128]{1,0:T(8,128)(2,1)} %bitcast.22), custom_call_target="tpu_custom_call" | custom-call | tf_op jit(solution)/shard_map/pack/pallas_call | solution.py:393
  3.8 0.0 copy-start
  3.8 0.0 copy-start.1
  3.8 0.0 copy-start.2
  3.8 0.0 copy-start.3
  3.8 0.0 copy-start.4
  3.8 0.0 copy-start.5
  3.8 15.7 %all-to-all-start = ((bf16[256,9,2,128]{3,2,1,0:T(2,128)(2,1)}), bf16[256,9,2,128]{3,2,1,0:T(2,128)(2,1)S(1)}, u32[]{:S(2)}, u32[]{:S(2)}) async-start(bf16[256,9,2,128]{3,2,1,0:T(2,128)(2,1)} %bitcast.20), calls=%async_computation | async-start | bytes 2359296 | tf_op jit(solution)/shard_map/all_to_all | solution.py:370
  19.5 0.0 copy-done
  19.5 0.0 copy-done.1
  19.5 0.0 copy-done.2
  19.5 0.0 copy-done.3
  19.5 0.0 copy-done.4
  19.6 0.0 copy-done.5
  19.6 1.2 %setup.1 = (f32[4,2048]{1,0:T(4,128)S(1)}, f32[48,2048]{1,0:T(8,128)S(1)}, f32[48,2048]{1,0:T(8,128)S(1)}, f32[48,2048]{1,0:T(8,128)S(1)}, f32[2,2048]{1,0:T(2,1...) custom-call(s32[1]{0:T(128)} %bitcast.1.me_ref, ...), custom_call_target="tpu_custom_call" | custom-call | tf_op jit(solution)/shard_map/setup/pallas_call | solution.py:410
  20.8 32.5 %all-to-all-done = bf16[256,9,2,128]{3,2,1,0:T(2,128)(2,1)S(1)} async-done(((bf16[256,9,2,128]{3,2,1,0:T(2,128)(2,1)}), bf16[256,9,2,128]{3,2,1,0:T(2,128)(2,1)S(1)}, u32[]{:S(2)}, u32[]{:S(2)}) %all-to-all-start) | async-done | bytes 1179680 | tf_op jit(solution)/shard_map/all_to_all | solution.py:370
  53.3 10.0 %owner.1 = bf16[4608,128]{1,0:T(8,128)(2,1)S(1)} custom-call(s32[1]{0:T(128)} %bitcast.1.me_ref, s32[2,32]{1,0:T(2,128)S(1)} %bitcast.16, bf16[4608,128]{1,0:T(8,128)(2,1)S(1)} %bitcast.11, bf16[2048,1024]{1,0:T(8,128)(2,1)} %bitcast.21, f32[4,2048]{1,0:T(4,128)S(1)} %get-tuple-element.13.links_ref, ...), custom_call_target="tpu_custom_call", output_to_operand_aliasing={{}: (2, {})} | custom-call | tf_op jit(solution)/shard_map/owner/pallas_call | solution.py:435
  63.3 39.6 %all_to_all.10 = bf16[256,9,2,128]{3,2,1,0:T(2,128)(2,1)S(1)} all-to-all(bf16[256,9,2,128]{3,2,1,0:T(2,128)(2,1)S(1)} %bitcast.12), channel_id=1, replica_groups=mesh['lat'=32,'mode'=8] {'lat','mode'}, dimensions={0} | all-to-all | bytes 2359296 | tf_op jit(solution)/shard_map/all_to_all | solution.py:370
  102.9 2.9 %unpack.1 = bf16[4608,128]{1,0:T(8,128)(2,1)} custom-call(s32[2,32]{1,0:T(2,128)S(1)} %bitcast.17, bf16[4608,128]{1,0:T(8,128)(2,1)S(1)} %bitcast.13), custom_call_target="tpu_custom_call" | custom-call | tf_op jit(solution)/shard_map/unpack/pallas_call | solution.py:456
Async XLA Ops:
  3.8 15.7 %copy-start = (f32[4,1,2048]{2,1,0:T(1,128)S(1)}, f32[4,1,2048]{2,1,0:T(1,128)}, u32[]{:S(2)}) copy-start(f32[4,1,2048]{2,1,0:T(1,128)} %coupling_ref.1) | copy-start | bytes 98308
  3.8 15.7 %copy-start.1 = (f32[48,48]{1,0:T(8,128)S(1)}, f32[48,48]{1,0:T(8,128)}, u32[]{:S(2)}) copy-start(f32[48,48]{1,0:T(8,128)} %into_ref.1) | copy-start | bytes 27652
  3.8 15.7 %copy-start.2 = (f32[48,48]{1,0:T(8,128)S(1)}, f32[48,48]{1,0:T(8,128)}, u32[]{:S(2)}) copy-start(f32[48,48]{1,0:T(8,128)} %out_of_ref.1) | copy-start | bytes 27652
  3.8 15.7 %copy-start.3 = (s32[32,2]{0,1:T(2,128)S(1)}, s32[32,2]{0,1:T(2,128)}, u32[]{:S(2)}) copy-start(s32[32,2]{0,1:T(2,128)} %param.9) | copy-start | bytes 772
  3.8 15.7 %copy-start.4 = (f32[48]{0:T(128)S(1)}, f32[48]{0:T(128)}, u32[]{:S(2)}) copy-start(f32[48]{0:T(128)} %param.12) | copy-start | bytes 580
  3.8 15.7 %copy-start.5 = (f32[48]{0:T(128)S(1)}, f32[48]{0:T(128)}, u32[]{:S(2)}) copy-start(f32[48]{0:T(128)} %param.13) | copy-start | bytes 580
  3.8 49.5 %all-to-all-start = ((bf16[256,9,2,128]{3,2,1,0:T(2,128)(2,1)}), bf16[256,9,2,128]{3,2,1,0:T(2,128)(2,1)S(1)}, u32[]{:S(2)}, u32[]{:S(2)}) async-start(bf16[256,9,2,128]{3,2,1,0:T(2,128)(2,1)} %bitcast.20), calls=%async_computation | async-start | bytes 2359296 | tf_op jit(solution)/shard_map/all_to_all | solution.py:370

commit v3 on v2

--- a/solution.py
+++ b/solution.py
@@ -43,11 +43,23 @@
 
 
 def pack_kernel(
-    table_ref, x_ref, out_ref, table, held, stage_ref, load_sem, table_sem, *, owners, window
+    table_ref,
+    x_ref,
+    out_ref,
+    table,
+    held,
+    stage_ref,
+    load_sem,
+    table_sem,
+    store_sem,
+    *,
+    owners,
+    window,
 ):
-    columns = x_ref.shape[0] // BAND
+    size = x_ref.shape[0]
+    columns = size // BAND
     loads = load_sem.shape[0]
-    part_rows = x_ref.shape[0] // loads
+    part_rows = size // loads
     fetch = pltpu.make_async_copy(table_ref, table, table_sem)
     fetch.start()
     copies = []
@@ -57,28 +69,35 @@
         copies[i].start()
     fetch.wait()
     selector = wave_selector(table, owners, window)
-    ready = 0
-    for pair in range(columns // 8):
-        while ready * part_rows < (pair + 1) * 256:
-            copies[ready].wait()
-            ready += 1
-        both = lax.dot_general(
+    for i in range(loads):
+        copies[i].wait()
+        whole = lax.dot_general(
             selector,
-            held[pair * 256 : (pair + 1) * 256, :],
+            held[i * part_rows : (i + 1) * part_rows, :],
             (((1,), (1,)), ((), ())),
             preferred_element_type=F32,
         ).astype(BF16)
-        for half in range(2):
-            turned = both[:, half * 128 : (half + 1) * 128]
-            parts = swap_blocks([turned[i * owners : (i + 1) * owners] for i in range(4)])
-            for i in range(4):
-                here = pl.ds(pair * 8 + half * 4 + i, owners, stride=columns + 1)
-                stage_ref[here, :] = parts[i].astype(F32)
+        for group in range(part_rows // 128):
+            turned = whole[:, group * 128 : (group + 1) * 128]
+            parts = swap_blocks([turned[k * owners : (k + 1) * owners] for k in range(4)])
+            for k in range(4):
+                column = i * (part_rows // BAND) + group * 4 + k
+                stage_ref[pl.ds(column, owners, stride=columns + 1), :] = parts[k].astype(F32)
+    stores = store_sem.shape[0]
+    each = owners // stores
+    sent = []
     for owner in range(owners):
         start = owner * (columns + 1)
-        out_ref[owner * columns : (owner + 1) * columns, :] = stage_ref[
+        held[owner * columns : (owner + 1) * columns, :] = stage_ref[
             start : start + columns, :
         ].astype(BF16)
+        if (owner + 1) % each == 0:
+            k = owner // each
+            here = pl.ds(k * each * columns, each * columns)
+            sent.append(pltpu.make_async_copy(held.at[here], out_ref.at[here], store_sem.at[k]))
+            sent[k].start()
+    for copy in sent:
+        copy.wait()
 
 
 def unpack_kernel(
@@ -101,9 +120,9 @@
         here = pl.ds(i * part_rows, part_rows)
         copies.append(pltpu.make_async_copy(held.at[here], out_ref.at[here], store_sem.at[i]))
     sent = 0
-    for first in range(0, columns // 4, 4):
+    for first in range(0, columns // 4, 12):
         upright = []
-        for group in range(first, first + 4):
+        for group in range(first, first + 12):
             parts = [
                 stage_ref[pl.ds(group * 4 + i, owners, stride=columns + 1), :].astype(BF16)
                 for i in range(4)
@@ -116,8 +135,8 @@
             )
         upright = jnp.concatenate(upright, axis=0).astype(BF16)
         rows = jnp.dot(upright, selector, preferred_element_type=F32)
-        held[first * 128 : (first + 4) * 128, :] = rows.astype(BF16)
-        while sent < stores and (sent + 1) * part_rows <= (first + 4) * 128:
+        held[first * 128 : (first + 12) * 128, :] = rows.astype(BF16)
+        while sent < stores and (sent + 1) * part_rows <= (first + 12) * 128:
             copies[sent].start()
             sent += 1
     for copy in copies:
@@ -164,7 +183,6 @@
     lines_ref,
     mix_in_ref,
     mix_out_ref,
-    mix_low_ref,
     *,
     window,
 ):
@@ -208,10 +226,14 @@
             mix_in.append(jnp.dot(into_parts[part], wide[field], preferred_element_type=F32))
             mix_out.append(jnp.dot(tall[field], out_parts[part], preferred_element_type=F32))
     mix_in_ref[...] = jnp.concatenate(mix_in, axis=0).astype(BF16)
+    none = jnp.zeros((cols, levels), F32)
     mix_out_ref[...] = jnp.concatenate(
-        [tall[0].astype(F32)] + mix_out[:2] + mix_out[:2], axis=1
+        [
+            jnp.concatenate([tall[0].astype(F32)] + mix_out[:2] + mix_out[:2], axis=1),
+            jnp.concatenate([none] + mix_out[2:] + [none, none], axis=1),
+        ],
+        axis=0,
     ).astype(BF16)
-    mix_low_ref[...] = jnp.concatenate(mix_out[2:], axis=1).astype(BF16)
 
 
 def owner_kernel(
@@ -226,7 +248,6 @@
     lines_ref,
     mix_in_ref,
     mix_out_ref,
-    mix_low_ref,
     out_ref,
     grid_ref,
     spec_ref,
@@ -243,12 +264,12 @@
     levels, rows = scale_ref.shape
     pairs = rows // 256
     loads = []
-    for pair in range(pairs):
-        here = pl.ds(pair * 256, 256)
+    for number, (start, count) in enumerate(((0, 1), (1, 1), (2, 2))):
+        here = pl.ds(start * (rows // 4), count * (rows // 4))
         loads.append(
-            pltpu.make_async_copy(source_ref.at[here], legendre_ref.at[here], load_sem.at[pair])
+            pltpu.make_async_copy(source_ref.at[here], legendre_ref.at[here], load_sem.at[number])
         )
-        loads[pair].start()
+        loads[number].start()
     cols = 3 * levels
     owners = q_ref.shape[0] // cols
     count0 = NN // BLK - (table_ref[0, me_ref[0]] * NN) // window // BLK
@@ -268,9 +289,8 @@
     for pair in range(pairs):
         here = slice(pair * 256, (pair + 1) * 256)
         slot = (2 * pair >= count0).astype(jnp.int32)
-        if pair in (0, 4):
-            for load in loads[pair : pair + 4]:
-                load.wait()
+        if pair * 4 in (0, pairs, 2 * pairs):
+            loads[pair * 4 // pairs].wait()
         found = lax.dot_general(
             grid_ref[slot], legendre_ref[here, :], nt, preferred_element_type=F32
         )
@@ -320,8 +340,10 @@
                 mix_out_ref[...],
                 jnp.concatenate([vort_ref[part, :, here], high, low], axis=0),
                 preferred_element_type=F32,
-            ) + jnp.dot(mix_low_ref[...], high, preferred_element_type=F32)
-            update_ref[part * cols : (part + 1) * cols, here] = mixed.astype(BF16)
+            )
+            update_ref[part * cols : (part + 1) * cols, here] = (
+                mixed[:cols] + mixed[cols:]
+            ).astype(BF16)
 
     for pair in (0, pairs - 1) + tuple(range(1, pairs - 1)):
         here = slice(pair * 256, (pair + 1) * 256)
@@ -394,13 +416,14 @@
         functools.partial(pack_kernel, owners=owners, window=window),
         out_shape=flat,
         in_specs=[HBM, HBM],
-        out_specs=VMEM,
+        out_specs=HBM,
         scratch_shapes=[
             pltpu.VMEM((2, owners), jnp.int32),
             pltpu.VMEM((size, LANES), BF16),
             pltpu.VMEM((staged, LANES), F32),
+            pltpu.SemaphoreType.DMA((2,)),
+            pltpu.SemaphoreType.DMA,
             pltpu.SemaphoreType.DMA((4,)),
-            pltpu.SemaphoreType.DMA,
         ],
         compiler_params=pltpu.CompilerParams(vmem_limit_bytes=60 * MIB),
         name="pack",
@@ -416,11 +439,10 @@
             jax.ShapeDtypeStruct((levels, rows), F32),
             jax.ShapeDtypeStruct((2, rows), F32),
             jax.ShapeDtypeStruct((5 * levels, cols), BF16),
-            jax.ShapeDtypeStruct((cols, 5 * levels), BF16),
-            jax.ShapeDtypeStruct((cols, 2 * levels), BF16),
+            jax.ShapeDtypeStruct((2 * cols, 5 * levels), BF16),
         ],
         in_specs=[SMEM, SMEM] + [VMEM] * 5,
-        out_specs=[VMEM] * 8,
+        out_specs=[VMEM] * 7,
         compiler_params=pltpu.CompilerParams(vmem_limit_bytes=16 * MIB),
         name="setup",
     )(
@@ -435,7 +457,7 @@
     synthesis = pl.pallas_call(
         functools.partial(owner_kernel, window=window),
         out_shape=flat,
-        in_specs=[SMEM, SMEM, VMEM, HBM] + [VMEM] * 8,
+        in_specs=[SMEM, SMEM, VMEM, HBM] + [VMEM] * 7,
         out_specs=VMEM,
         scratch_shapes=[
             pltpu.VMEM((2, 2 * cols, latitudes), BF16),
@@ -446,7 +468,7 @@
             pltpu.VMEM((2 * cols, rows), BF16),
             pltpu.VMEM((2, 2 * cols, latitudes), F32),
             pltpu.VMEM((rows, latitudes), BF16),
-            pltpu.SemaphoreType.DMA((rows // 256,)),
+            pltpu.SemaphoreType.DMA((3,)),
         ],
         input_output_aliases={2: 0},
         compiler_params=pltpu.CompilerParams(vmem_limit_bytes=48 * MIB),

time: 106 us -> 105 us (level)
  Pallas kernels: 17.8 us -> 15.6 us
    pallas_call x1, Pallas kernels: 9.97 us -> 8.61 us  [body(): pl.pallas_call(functools.partial(owner_kernel, window=window), out_shape=...]
where the time goes in v3:
time: 105 us; the launch traced here: 104 us
  blocking collectives  40.4 us (38%)
  waiting for transfers between devices  32.5 us (31%)
  starting transfers between devices  15.7 us (15%)
  Pallas kernels  15.6 us (15%)
    all_to_all x1, blocking collectives, exchange(): lax.all_to_all(chunks, ('lat', 'mode'), 0, 0, tiled=True)  40.4 us
    all_to_all x1, waiting for transfers between devices, exchange(): lax.all_to_all(chunks, ('lat', 'mode'), 0, 0, tiled=True)  32.5 us
    all_to_all x1, starting transfers between devices, exchange(): lax.all_to_all(chunks, ('lat', 'mode'), 0, 0, tiled=True)  15.7 us
    pallas_call x1, Pallas kernels, body(): pl.pallas_call(functools.partial(owner_kernel, window=window), out_shape=...  8.61 us
    pallas_call x1, Pallas kernels, body(): pl.pallas_call(functools.partial(pack_kernel, owners=owners, window=windo...  3.29 us
    pallas_call x1, Pallas kernels, body(): pl.pallas_call(functools.partial(unpack_kernel, owners=owners, window=win...  2.47 us
  transfers between devices with their start and end apart: 1, of which 1 were waited for; matrix products, arithmetic and copies ran while one was open for 0% of the time, Pallas kernels for 1%

profile of v3, /device:TPU:1, one launch (start us, length us, event | category | flops | bytes accessed | tf_op | source)
XLA Modules:
  0.0 104.4 jit_solution(10384317463712601852)
XLA Ops:
  0.0 3.3 %pack.1 = bf16[4608,128]{1,0:T(8,128)(2,1)} custom-call(s32[2,32]{1,0:T(2,128)} %bitcast.14, bf16[4608,128]{1,0:T(8,128)(2,1)} %bitcast.22), custom_call_target="tpu_custom_call" | custom-call | tf_op jit(solution)/shard_map/pack/pallas_call | solution.py:415
  3.3 0.0 copy-start
  3.3 0.0 copy-start.1
  3.3 0.0 copy-start.2
  3.3 0.0 copy-start.3
  3.4 0.0 copy-start.4
  3.4 0.0 copy-start.5
  3.4 15.7 %all-to-all-start = ((bf16[256,9,2,128]{3,2,1,0:T(2,128)(2,1)}), bf16[256,9,2,128]{3,2,1,0:T(2,128)(2,1)S(1)}, u32[]{:S(2)}, u32[]{:S(2)}) async-start(bf16[256,9,2,128]{3,2,1,0:T(2,128)(2,1)} %bitcast.20), calls=%async_computation | async-start | bytes 2359296 | tf_op jit(solution)/shard_map/all_to_all | solution.py:392
  19.1 0.0 copy-done
  19.1 0.0 copy-done.1
  19.1 0.0 copy-done.2
  19.1 0.0 copy-done.3
  19.1 0.0 copy-done.4
  19.1 0.0 copy-done.5
  19.1 1.2 %setup.1 = (f32[4,2048]{1,0:T(4,128)S(1)}, f32[48,2048]{1,0:T(8,128)S(1)}, f32[48,2048]{1,0:T(8,128)S(1)}, f32[48,2048]{1,0:T(8,128)S(1)}, f32[2,2048]{1,0:T(2,1...) custom-call(s32[1]{0:T(128)} %bitcast.1.me_ref, s32[2,32]{1,0:T(2,128)S(1)} %bitcast.15, ...), custom_call_target="tpu_custom_call" | custom-call | tf_op jit(solution)/shard_map/setup/pallas_call | solution.py:433
  20.3 32.5 %all-to-all-done = bf16[256,9,2,128]{3,2,1,0:T(2,128)(2,1)S(1)} async-done(((bf16[256,9,2,128]{3,2,1,0:T(2,128)(2,1)}), bf16[256,9,2,128]{3,2,1,0:T(2,128)(2,1)S(1)}, u32[]{:S(2)}, u32[]{:S(2)}) %all-to-all-start) | async-done | bytes 1179680 | tf_op jit(solution)/shard_map/all_to_all | solution.py:392
  52.9 8.6 %owner.1 = bf16[4608,128]{1,0:T(8,128)(2,1)S(1)} custom-call(s32[1]{0:T(128)} %bitcast.1.me_ref, s32[2,32]{1,0:T(2,128)S(1)} %bitcast.16, bf16[4608,128]{1,0:T(8,128)(2,1)S(1)} %bitcast.11, bf16[2048,1024]{1,0:T(8,128)(2,1)} %bitcast.21, f32[4,2048]{1,0:T(4,128)S(1)} %get-tuple-element.12.links_ref, ...), custom_call_target="tpu_custom_call", output_to_operand_aliasing={{}: (2, {})} | custom-call | tf_op jit(solution)/shard_map/owner/pallas_call | solution.py:457
  61.5 40.4 %all_to_all.10 = bf16[256,9,2,128]{3,2,1,0:T(2,128)(2,1)S(1)} all-to-all(bf16[256,9,2,128]{3,2,1,0:T(2,128)(2,1)S(1)} %bitcast.12), channel_id=1, replica_groups=mesh['lat'=32,'mode'=8] {'lat','mode'}, dimensions={0} | all-to-all | bytes 2359296 | tf_op jit(solution)/shard_map/all_to_all | solution.py:392
  101.9 2.5 %unpack.1 = bf16[4608,128]{1,0:T(8,128)(2,1)} custom-call(s32[2,32]{1,0:T(2,128)S(1)} %bitcast.17, bf16[4608,128]{1,0:T(8,128)(2,1)S(1)} %bitcast.13), custom_call_target="tpu_custom_call" | custom-call | tf_op jit(solution)/shard_map/unpack/pallas_call | solution.py:478
Async XLA Ops:
  3.3 15.8 %copy-start = (f32[4,1,2048]{2,1,0:T(1,128)S(1)}, f32[4,1,2048]{2,1,0:T(1,128)}, u32[]{:S(2)}) copy-start(f32[4,1,2048]{2,1,0:T(1,128)} %coupling_ref.1) | copy-start | bytes 98308
  3.3 15.7 %copy-start.1 = (f32[48,48]{1,0:T(8,128)S(1)}, f32[48,48]{1,0:T(8,128)}, u32[]{:S(2)}) copy-start(f32[48,48]{1,0:T(8,128)} %into_ref.1) | copy-start | bytes 27652
  3.3 15.7 %copy-start.2 = (f32[48,48]{1,0:T(8,128)S(1)}, f32[48,48]{1,0:T(8,128)}, u32[]{:S(2)}) copy-start(f32[48,48]{1,0:T(8,128)} %out_of_ref.1) | copy-start | bytes 27652
  3.3 15.7 %copy-start.3 = (s32[32,2]{0,1:T(2,128)S(1)}, s32[32,2]{0,1:T(2,128)}, u32[]{:S(2)}) copy-start(s32[32,2]{0,1:T(2,128)} %param.9) | copy-start | bytes 772
  3.4 15.7 %copy-start.4 = (f32[48]{0:T(128)S(1)}, f32[48]{0:T(128)}, u32[]{:S(2)}) copy-start(f32[48]{0:T(128)} %param.12) | copy-start | bytes 580
  3.4 15.7 %copy-start.5 = (f32[48]{0:T(128)S(1)}, f32[48]{0:T(128)}, u32[]{:S(2)}) copy-start(f32[48]{0:T(128)} %param.13) | copy-start | bytes 580
  3.4 49.5 %all-to-all-start = ((bf16[256,9,2,128]{3,2,1,0:T(2,128)(2,1)}), bf16[256,9,2,128]{3,2,1,0:T(2,128)(2,1)S(1)}, u32[]{:S(2)}, u32[]{:S(2)}) async-start(bf16[256,9,2,128]{3,2,1,0:T(2,128)(2,1)} %bitcast.20), calls=%async_computation | async-start | bytes 2359296 | tf_op jit(solution)/shard_map/all_to_all | solution.py:392

commit v4 on v3

--- a/solution.py
+++ b/solution.py
@@ -171,21 +171,26 @@
 def setup_kernel(
     me_ref,
     table_ref,
+    legendre_ref,
     coupling_ref,
     gravity_ref,
     hyper_ref,
     into_ref,
     out_of_ref,
+    lead_ref,
     links_ref,
-    scale_ref,
-    inverse_ref,
-    damped_ref,
+    columns_ref,
     lines_ref,
     mix_in_ref,
     mix_out_ref,
+    load_sem,
     *,
     window,
 ):
+    load = pltpu.make_async_copy(
+        legendre_ref.at[pl.ds(0, lead_ref.shape[0])], lead_ref, load_sem
+    )
+    load.start()
     rows = coupling_ref.shape[2]
     levels = gravity_ref.shape[1]
     cols = 3 * levels
@@ -202,13 +207,9 @@
         inside = jnp.logical_and(index + distance >= 0, index + distance < rows)
         joined = jnp.logical_and(joined, inside)
         links_ref[number : number + 1, :] = jnp.where(joined[:1], coupling_ref[number], 0.0)
-    gravity = column_of(gravity_ref[...], levels)
-    hyper = column_of(hyper_ref[...], levels)
-    weighted = gravity * wave_factor[:1]
-    inverse = usable_f[:1] / (1.0 + weighted)
-    scale_ref[...] = weighted * inverse
-    inverse_ref[...] = inverse
-    damped_ref[...] = usable_f[:1] / (1.0 + hyper * (wave_factor[:1] * wave_factor[:1]))
+    wide_shape = (levels, LANES)
+    columns_ref[0] = jnp.broadcast_to(column_of(gravity_ref[...], levels), wide_shape)
+    columns_ref[1] = jnp.broadcast_to(column_of(hyper_ref[...], levels), wide_shape)
 
     wide_row = lax.broadcasted_iota(jnp.int32, (levels, cols), 0)
     wide_col = lax.broadcasted_iota(jnp.int32, (levels, cols), 1)
@@ -234,6 +235,7 @@
         ],
         axis=0,
     ).astype(BF16)
+    load.wait()
 
 
 def owner_kernel(
@@ -241,10 +243,9 @@
     table_ref,
     q_ref,
     source_ref,
+    lead_ref,
     links_ref,
-    scale_ref,
-    inverse_ref,
-    damped_ref,
+    columns_ref,
     lines_ref,
     mix_in_ref,
     mix_out_ref,
@@ -257,15 +258,17 @@
     update_ref,
     total_ref,
     legendre_ref,
+    inverse_ref,
+    damped_ref,
     load_sem,
     *,
     window,
 ):
-    levels, rows = scale_ref.shape
+    levels, rows = inverse_ref.shape
     pairs = rows // 256
     loads = []
-    for number, (start, count) in enumerate(((0, 1), (1, 1), (2, 2))):
-        here = pl.ds(start * (rows // 4), count * (rows // 4))
+    for number, (start, count) in enumerate(((3, 2), (5, 3))):
+        here = pl.ds(start * (rows // 8), count * (rows // 8))
         loads.append(
             pltpu.make_async_copy(source_ref.at[here], legendre_ref.at[here], load_sem.at[number])
         )
@@ -273,8 +276,13 @@
     cols = 3 * levels
     owners = q_ref.shape[0] // cols
     count0 = NN // BLK - (table_ref[0, me_ref[0]] * NN) // window // BLK
-    straddles = count0 % 2 == 1
     cut = pl.multiple_of(count0 * BLK, BLK)
+
+    legendre_ref[: rows // 8 * 3, :] = lead_ref[...]
+
+    factor, usable = lines_ref[0:1, :], lines_ref[1:2, :]
+    inverse_ref[...] = usable / (1.0 + columns_ref[0, :, :1] * factor)
+    damped_ref[...] = usable / (1.0 + columns_ref[1, :, :1] * (factor * factor))
 
     for group in range(owners // 4):
         parts = [q_ref[(group * 4 + i) * cols : (group * 4 + i + 1) * cols, :] for i in range(4)]
@@ -289,19 +297,17 @@
     for pair in range(pairs):
         here = slice(pair * 256, (pair + 1) * 256)
         slot = (2 * pair >= count0).astype(jnp.int32)
-        if pair * 4 in (0, pairs, 2 * pairs):
-            loads[pair * 4 // pairs].wait()
+        if pair * 8 in (3 * pairs, 5 * pairs):
+            loads[int(pair * 8 == 5 * pairs)].wait()
         found = lax.dot_general(
             grid_ref[slot], legendre_ref[here, :], nt, preferred_element_type=F32
         )
         spec_ref[:, here] = (found * lines_ref[1:2, here]).astype(BF16)
 
-    @pl.when(straddles)
-    def _():
-        found = lax.dot_general(
-            grid_ref[1], legendre_ref[pl.ds(cut, BLK), :], nt, preferred_element_type=F32
-        )
-        spec_ref[:, pl.ds(cut, BLK)] = (found * lines_ref[1:2, pl.ds(cut, BLK)]).astype(BF16)
+    found = lax.dot_general(
+        grid_ref[1], legendre_ref[pl.ds(cut, BLK), :], nt, preferred_element_type=F32
+    )
+    spec_ref[:, pl.ds(cut, BLK)] = (found * lines_ref[1:2, pl.ds(cut, BLK)]).astype(BF16)
 
     for part in range(2):
         for pair in range(pairs):
@@ -327,7 +333,7 @@
                 around = around + links_ref[1 : 2, :] * pltpu.roll(answer, 1, 1)
                 around = around + links_ref[2 : 3, :] * pltpu.roll(answer, rows - 1, 1)
                 around = around + links_ref[3 : 4, :] * pltpu.roll(answer, rows - 2, 1)
-                answer = right - scale_ref[mine, :] * around
+                answer = right - (1.0 - inverse_ref[mine, :]) * around
             right_ref[part, mine, :] = answer
 
     for pair in range(pairs):
@@ -345,28 +351,22 @@
                 mixed[:cols] + mixed[cols:]
             ).astype(BF16)
 
+    alone = jnp.dot(
+        update_ref[:, pl.ds(cut, BLK)], legendre_ref[pl.ds(cut, BLK), :], preferred_element_type=F32
+    )
     for pair in (0, pairs - 1) + tuple(range(1, pairs - 1)):
         here = slice(pair * 256, (pair + 1) * 256)
         slot = (2 * pair >= count0).astype(jnp.int32)
         values = update_ref[:, here]
-        spills = count0 == 2 * pair + 1
-        lane = lax.broadcasted_iota(jnp.int32, values.shape, 1)
-        values = jnp.where(jnp.logical_and(spills, lane >= BLK), jnp.zeros_like(values), values)
+        block = 2 * pair + lax.broadcasted_iota(jnp.int32, values.shape, 1) // BLK
+        values = jnp.where(block == count0, jnp.zeros_like(values), values)
         term = jnp.dot(values, legendre_ref[here, :], preferred_element_type=F32)
         if pair == 0:
             total_ref[0] = term
         elif pair == pairs - 1:
-            total_ref[1] = term
+            total_ref[1] = term + alone
         else:
             total_ref[slot] += term
-
-    @pl.when(straddles)
-    def _():
-        total_ref[1] += jnp.dot(
-            update_ref[:, pl.ds(cut, BLK)],
-            legendre_ref[pl.ds(cut, BLK), :],
-            preferred_element_type=F32,
-        )
 
     for group in range(owners // 4):
         parts = [
@@ -433,21 +433,22 @@
     prepared = pl.pallas_call(
         functools.partial(setup_kernel, window=window),
         out_shape=[
+            jax.ShapeDtypeStruct((rows // 8 * 3, latitudes), BF16),
             jax.ShapeDtypeStruct((4, rows), F32),
-            jax.ShapeDtypeStruct((levels, rows), F32),
-            jax.ShapeDtypeStruct((levels, rows), F32),
-            jax.ShapeDtypeStruct((levels, rows), F32),
+            jax.ShapeDtypeStruct((2, levels, LANES), F32),
             jax.ShapeDtypeStruct((2, rows), F32),
             jax.ShapeDtypeStruct((5 * levels, cols), BF16),
             jax.ShapeDtypeStruct((2 * cols, 5 * levels), BF16),
         ],
-        in_specs=[SMEM, SMEM] + [VMEM] * 5,
-        out_specs=[VMEM] * 7,
+        in_specs=[SMEM, SMEM, HBM] + [VMEM] * 5,
+        out_specs=[VMEM] * 6,
+        scratch_shapes=[pltpu.SemaphoreType.DMA],
         compiler_params=pltpu.CompilerParams(vmem_limit_bytes=16 * MIB),
         name="setup",
     )(
         me,
         table,
+        legendre.reshape(rows, latitudes),
         coupling,
         gravity.reshape(1, levels),
         hyper_diff.reshape(1, levels),
@@ -457,7 +458,7 @@
     synthesis = pl.pallas_call(
         functools.partial(owner_kernel, window=window),
         out_shape=flat,
-        in_specs=[SMEM, SMEM, VMEM, HBM] + [VMEM] * 7,
+        in_specs=[SMEM, SMEM, VMEM, HBM] + [VMEM] * 6,
         out_specs=VMEM,
         scratch_shapes=[
             pltpu.VMEM((2, 2 * cols, latitudes), BF16),
@@ -468,7 +469,9 @@
             pltpu.VMEM((2 * cols, rows), BF16),
             pltpu.VMEM((2, 2 * cols, latitudes), F32),
             pltpu.VMEM((rows, latitudes), BF16),
-            pltpu.SemaphoreType.DMA((3,)),
+            pltpu.VMEM((levels, rows), F32),
+            pltpu.VMEM((levels, rows), F32),
+            pltpu.SemaphoreType.DMA((2,)),
         ],
         input_output_aliases={2: 0},
         compiler_params=pltpu.CompilerParams(vmem_limit_bytes=48 * MIB),

time: 105 us -> 104 us (level)
  waiting for transfers between devices: 32.5 us -> 30.3 us
  local copies, waits for them, and re-layouts: 0.04 us -> 2.22 us
    all_to_all x1, waiting for transfers between devices: 32.5 us -> 30.3 us  [exchange(): lax.all_to_all(chunks, ('lat', 'mode'), 0, 0, tiled=True)]
    unnamed x12 -> x14, local copies, waits for them, and re-layouts: 0.04 us -> 2.22 us
where the time goes in v4:
time: 104 us; the launch traced here: 103 us
  blocking collectives  40 us (38%)
  waiting for transfers between devices  30.3 us (29%)
  starting transfers between devices  15.7 us (15%)
  Pallas kernels  15 us (14%)
  local copies, waits for them, and re-layouts  2.22 us (2%)
    all_to_all x1, blocking collectives, exchange(): lax.all_to_all(chunks, ('lat', 'mode'), 0, 0, tiled=True)  40 us
    all_to_all x1, waiting for transfers between devices, exchange(): lax.all_to_all(chunks, ('lat', 'mode'), 0, 0, tiled=True)  30.3 us
    all_to_all x1, starting transfers between devices, exchange(): lax.all_to_all(chunks, ('lat', 'mode'), 0, 0, tiled=True)  15.7 us
    pallas_call x1, Pallas kernels, body(): pl.pallas_call(functools.partial(owner_kernel, window=window), out_shape=...  8.01 us
    pallas_call x1, Pallas kernels, body(): pl.pallas_call(functools.partial(pack_kernel, owners=owners, window=windo...  3.29 us
    pallas_call x1, Pallas kernels, body(): pl.pallas_call(functools.partial(unpack_kernel, owners=owners, window=win...  2.47 us
    unnamed x14, local copies, waits for them, and re-layouts  2.22 us
  transfers between devices with their start and end apart: 1, of which 1 were waited for; matrix products, arithmetic and copies ran while one was open for 0% of the time, Pallas kernels for 1%

profile of v4, /device:TPU:1, one launch (start us, length us, event | category | flops | bytes accessed | tf_op | source)
XLA Modules:
  0.0 103.3 jit_solution(1943100969789785469)
XLA Ops:
  0.0 3.3 %pack.1 = bf16[4608,128]{1,0:T(8,128)(2,1)} custom-call(s32[2,32]{1,0:T(2,128)} %bitcast.16, bf16[4608,128]{1,0:T(8,128)(2,1)} %bitcast.23), custom_call_target="tpu_custom_call" | custom-call | tf_op jit(solution)/shard_map/pack/pallas_call | solution.py:415
  3.3 0.0 copy-start.1
  3.3 0.0 copy-start.2
  3.3 0.0 copy-start.3
  3.3 0.0 copy-start.4
  3.4 0.0 copy-start.5
  3.4 0.0 copy-start.6
  3.4 15.7 %all-to-all-start = ((bf16[256,9,2,128]{3,2,1,0:T(2,128)(2,1)}), bf16[256,9,2,128]{3,2,1,0:T(2,128)(2,1)S(1)}, u32[]{:S(2)}, u32[]{:S(2)}) async-start(bf16[256,9,2,128]{3,2,1,0:T(2,128)(2,1)} %bitcast.22), calls=%async_computation | async-start | bytes 2359296 | tf_op jit(solution)/shard_map/all_to_all | solution.py:392
  19.1 0.0 copy-done.1
  19.1 0.0 copy-done.2
  19.1 0.0 copy-done.3
  19.1 0.0 copy-done.4
  19.1 0.0 copy-done.5
  19.1 0.0 copy-done.6
  19.1 0.0 copy-start
  19.1 2.2 %copy-done = bf16[1,16,128,1024]{3,2,1,0:T(8,128)(2,1)S(1)} copy-done((bf16[1,16,128,1024]{3,2,1,0:T(8,128)(2,1)S(1)}, bf16[1,16,128,1024]{3,2,1,0:T(8,128)(2,1)}, u32[]{:S(2)}) %copy-start) | copy-done | bytes 4194328
  21.3 1.3 %setup.1 = (bf16[768,1024]{1,0:T(8,128)(2,1)S(1)}, f32[4,2048]{1,0:T(4,128)S(1)}, f32[2,48,128]{2,1,0:T(8,128)S(1)}, f32[2,2048]{1,0:T(2,128)S(1)}, bf16[240,144...) custom-call(s32[1]{0:T(128)} %bitcast.1.me_ref, s32[2,32]{1,0:T(2,128)S(1)} %bitcast.17, bf16[2048,1024]{1,0:T(8,128)(2,1)S(1)} %bitcast.12, ...), custom_call_target="tpu_custom_call" | custom-call | tf_op jit(solution)/shard_map/setup/pallas_call | solution.py:433
  22.6 30.3 %all-to-all-done = bf16[256,9,2,128]{3,2,1,0:T(2,128)(2,1)S(1)} async-done(((bf16[256,9,2,128]{3,2,1,0:T(2,128)(2,1)}), bf16[256,9,2,128]{3,2,1,0:T(2,128)(2,1)S(1)}, u32[]{:S(2)}, u32[]{:S(2)}) %all-to-all-start) | async-done | bytes 1179680 | tf_op jit(solution)/shard_map/all_to_all | solution.py:392
  52.9 8.0 %owner.1 = bf16[4608,128]{1,0:T(8,128)(2,1)S(1)} custom-call(s32[1]{0:T(128)} %bitcast.1.me_ref, s32[2,32]{1,0:T(2,128)S(1)} %bitcast.18, bf16[4608,128]{1,0:T(8,128)(2,1)S(1)} %bitcast.13, bf16[2048,1024]{1,0:T(8,128)(2,1)} %bitcast.11, bf16[768,1024]{1,0:T(8,128)(2,1)S(1)} %get-tuple-element.11.lead_ref, ...), custom_call_target="tpu_custom_call", output_to_operand_aliasing={{}: (2, {})} | custom-call | tf_op jit(solution)/shard_map/owner/pallas_call | solution.py:458
  60.9 40.0 %all_to_all.10 = bf16[256,9,2,128]{3,2,1,0:T(2,128)(2,1)S(1)} all-to-all(bf16[256,9,2,128]{3,2,1,0:T(2,128)(2,1)S(1)} %bitcast.14), channel_id=1, replica_groups=mesh['lat'=32,'mode'=8] {'lat','mode'}, dimensions={0} | all-to-all | bytes 2359296 | tf_op jit(solution)/shard_map/all_to_all | solution.py:392
  100.8 2.5 %unpack.1 = bf16[4608,128]{1,0:T(8,128)(2,1)} custom-call(s32[2,32]{1,0:T(2,128)S(1)} %bitcast.19, bf16[4608,128]{1,0:T(8,128)(2,1)S(1)} %bitcast.15), custom_call_target="tpu_custom_call" | custom-call | tf_op jit(solution)/shard_map/unpack/pallas_call | solution.py:481
Async XLA Ops:
  3.3 15.8 %copy-start.1 = (f32[4,1,2048]{2,1,0:T(1,128)S(1)}, f32[4,1,2048]{2,1,0:T(1,128)}, u32[]{:S(2)}) copy-start(f32[4,1,2048]{2,1,0:T(1,128)} %coupling_ref.1) | copy-start | bytes 98308
  3.3 15.7 %copy-start.2 = (f32[48,48]{1,0:T(8,128)S(1)}, f32[48,48]{1,0:T(8,128)}, u32[]{:S(2)}) copy-start(f32[48,48]{1,0:T(8,128)} %into_ref.1) | copy-start | bytes 27652
  3.3 15.7 %copy-start.3 = (f32[48,48]{1,0:T(8,128)S(1)}, f32[48,48]{1,0:T(8,128)}, u32[]{:S(2)}) copy-start(f32[48,48]{1,0:T(8,128)} %out_of_ref.1) | copy-start | bytes 27652
  3.3 15.7 %copy-start.4 = (s32[32,2]{0,1:T(2,128)S(1)}, s32[32,2]{0,1:T(2,128)}, u32[]{:S(2)}) copy-start(s32[32,2]{0,1:T(2,128)} %param.9) | copy-start | bytes 772
  3.4 15.7 %copy-start.5 = (f32[48]{0:T(128)S(1)}, f32[48]{0:T(128)}, u32[]{:S(2)}) copy-start(f32[48]{0:T(128)} %param.12) | copy-start | bytes 580
  3.4 15.7 %copy-start.6 = (f32[48]{0:T(128)S(1)}, f32[48]{0:T(128)}, u32[]{:S(2)}) copy-start(f32[48]{0:T(128)} %param.13) | copy-start | bytes 580
  3.4 49.5 %all-to-all-start = ((bf16[256,9,2,128]{3,2,1,0:T(2,128)(2,1)}), bf16[256,9,2,128]{3,2,1,0:T(2,128)(2,1)S(1)}, u32[]{:S(2)}, u32[]{:S(2)}) async-start(bf16[256,9,2,128]{3,2,1,0:T(2,128)(2,1)} %bitcast.22), calls=%async_computation | async-start | bytes 2359296 | tf_op jit(solution)/shard_map/all_to_all | solution.py:392
  19.1 2.2 %copy-start = (bf16[1,16,128,1024]{3,2,1,0:T(8,128)(2,1)S(1)}, bf16[1,16,128,1024]{3,2,1,0:T(8,128)(2,1)}, u32[]{:S(2)}) copy-start(bf16[1,16,128,1024]{3,2,1,0:T(8,128)(2,1)} %param.10) | copy-start | bytes 12582916

commit v5 on v4

--- a/solution.py
+++ b/solution.py
@@ -354,12 +354,11 @@
     alone = jnp.dot(
         update_ref[:, pl.ds(cut, BLK)], legendre_ref[pl.ds(cut, BLK), :], preferred_element_type=F32
     )
+    update_ref[:, pl.ds(cut, BLK)] = jnp.zeros((2 * cols, BLK), BF16)
     for pair in (0, pairs - 1) + tuple(range(1, pairs - 1)):
         here = slice(pair * 256, (pair + 1) * 256)
         slot = (2 * pair >= count0).astype(jnp.int32)
         values = update_ref[:, here]
-        block = 2 * pair + lax.broadcasted_iota(jnp.int32, values.shape, 1) // BLK
-        values = jnp.where(block == count0, jnp.zeros_like(values), values)
         term = jnp.dot(values, legendre_ref[here, :], preferred_element_type=F32)
         if pair == 0:
             total_ref[0] = term

time: 104 us -> 104 us (level)
  no operation moved by 1% of the time
where the time goes in v5:
time: 104 us; the launch traced here: 103 us
  blocking collectives  40 us (38%)
  waiting for transfers between devices  30.3 us (29%)
  starting transfers between devices  15.7 us (15%)
  Pallas kernels  15 us (14%)
  local copies, waits for them, and re-layouts  2.22 us (2%)
    all_to_all x1, blocking collectives, exchange(): lax.all_to_all(chunks, ('lat', 'mode'), 0, 0, tiled=True)  40 us
    all_to_all x1, waiting for transfers between devices, exchange(): lax.all_to_all(chunks, ('lat', 'mode'), 0, 0, tiled=True)  30.3 us
    all_to_all x1, starting transfers between devices, exchange(): lax.all_to_all(chunks, ('lat', 'mode'), 0, 0, tiled=True)  15.7 us
    pallas_call x1, Pallas kernels, body(): pl.pallas_call(functools.partial(owner_kernel, window=window), out_shape=...  8.01 us
    pallas_call x1, Pallas kernels, body(): pl.pallas_call(functools.partial(pack_kernel, owners=owners, window=windo...  3.29 us
    pallas_call x1, Pallas kernels, body(): pl.pallas_call(functools.partial(unpack_kernel, owners=owners, window=win...  2.47 us
    unnamed x14, local copies, waits for them, and re-layouts  2.22 us
  transfers between devices with their start and end apart: 1, of which 1 were waited for; matrix products, arithmetic and copies ran while one was open for 0% of the time, Pallas kernels for 1%

profile of v5, /device:TPU:1, one launch (start us, length us, event | category | flops | bytes accessed | tf_op | source)
XLA Modules:
  0.0 103.3 jit_solution(6195225104869164702)
XLA Ops:
  0.0 3.3 %pack.1 = bf16[4608,128]{1,0:T(8,128)(2,1)} custom-call(s32[2,32]{1,0:T(2,128)} %bitcast.16, bf16[4608,128]{1,0:T(8,128)(2,1)} %bitcast.23), custom_call_target="tpu_custom_call" | custom-call | tf_op jit(solution)/shard_map/pack/pallas_call | solution.py:414
  3.3 0.0 copy-start.1
  3.3 0.0 copy-start.2
  3.3 0.0 copy-start.3
  3.3 0.0 copy-start.4
  3.4 0.0 copy-start.5
  3.4 0.0 copy-start.6
  3.4 15.7 %all-to-all-start = ((bf16[256,9,2,128]{3,2,1,0:T(2,128)(2,1)}), bf16[256,9,2,128]{3,2,1,0:T(2,128)(2,1)S(1)}, u32[]{:S(2)}, u32[]{:S(2)}) async-start(bf16[256,9,2,128]{3,2,1,0:T(2,128)(2,1)} %bitcast.22), calls=%async_computation | async-start | bytes 2359296 | tf_op jit(solution)/shard_map/all_to_all | solution.py:391
  19.1 0.0 copy-done.1
  19.1 0.0 copy-done.2
  19.1 0.0 copy-done.3
  19.1 0.0 copy-done.4
  19.1 0.0 copy-done.5
  19.1 0.0 copy-done.6
  19.1 0.0 copy-start
  19.1 2.2 %copy-done = bf16[1,16,128,1024]{3,2,1,0:T(8,128)(2,1)S(1)} copy-done((bf16[1,16,128,1024]{3,2,1,0:T(8,128)(2,1)S(1)}, bf16[1,16,128,1024]{3,2,1,0:T(8,128)(2,1)}, u32[]{:S(2)}) %copy-start) | copy-done | bytes 4194328
  21.3 1.3 %setup.1 = (bf16[768,1024]{1,0:T(8,128)(2,1)S(1)}, f32[4,2048]{1,0:T(4,128)S(1)}, f32[2,48,128]{2,1,0:T(8,128)S(1)}, f32[2,2048]{1,0:T(2,128)S(1)}, bf16[240,144...) custom-call(s32[1]{0:T(128)} %bitcast.1.me_ref, s32[2,32]{1,0:T(2,128)S(1)} %bitcast.17, bf16[2048,1024]{1,0:T(8,128)(2,1)S(1)} %bitcast.12, ...), custom_call_target="tpu_custom_call" | custom-call | tf_op jit(solution)/shard_map/setup/pallas_call | solution.py:432
  22.6 30.3 %all-to-all-done = bf16[256,9,2,128]{3,2,1,0:T(2,128)(2,1)S(1)} async-done(((bf16[256,9,2,128]{3,2,1,0:T(2,128)(2,1)}), bf16[256,9,2,128]{3,2,1,0:T(2,128)(2,1)S(1)}, u32[]{:S(2)}, u32[]{:S(2)}) %all-to-all-start) | async-done | bytes 1179680 | tf_op jit(solution)/shard_map/all_to_all | solution.py:391
  52.9 8.0 %owner.1 = bf16[4608,128]{1,0:T(8,128)(2,1)S(1)} custom-call(s32[1]{0:T(128)} %bitcast.1.me_ref, s32[2,32]{1,0:T(2,128)S(1)} %bitcast.18, bf16[4608,128]{1,0:T(8,128)(2,1)S(1)} %bitcast.13, bf16[2048,1024]{1,0:T(8,128)(2,1)} %bitcast.11, bf16[768,1024]{1,0:T(8,128)(2,1)S(1)} %get-tuple-element.11.lead_ref, ...), custom_call_target="tpu_custom_call", output_to_operand_aliasing={{}: (2, {})} | custom-call | tf_op jit(solution)/shard_map/owner/pallas_call | solution.py:457
  60.9 40.0 %all_to_all.10 = bf16[256,9,2,128]{3,2,1,0:T(2,128)(2,1)S(1)} all-to-all(bf16[256,9,2,128]{3,2,1,0:T(2,128)(2,1)S(1)} %bitcast.14), channel_id=1, replica_groups=mesh['lat'=32,'mode'=8] {'lat','mode'}, dimensions={0} | all-to-all | bytes 2359296 | tf_op jit(solution)/shard_map/all_to_all | solution.py:391
  100.9 2.5 %unpack.1 = bf16[4608,128]{1,0:T(8,128)(2,1)} custom-call(s32[2,32]{1,0:T(2,128)S(1)} %bitcast.19, bf16[4608,128]{1,0:T(8,128)(2,1)S(1)} %bitcast.15), custom_call_target="tpu_custom_call" | custom-call | tf_op jit(solution)/shard_map/unpack/pallas_call | solution.py:480
Async XLA Ops:
  3.3 15.8 %copy-start.1 = (f32[4,1,2048]{2,1,0:T(1,128)S(1)}, f32[4,1,2048]{2,1,0:T(1,128)}, u32[]{:S(2)}) copy-start(f32[4,1,2048]{2,1,0:T(1,128)} %coupling_ref.1) | copy-start | bytes 98308
  3.3 15.7 %copy-start.2 = (f32[48,48]{1,0:T(8,128)S(1)}, f32[48,48]{1,0:T(8,128)}, u32[]{:S(2)}) copy-start(f32[48,48]{1,0:T(8,128)} %into_ref.1) | copy-start | bytes 27652
  3.3 15.7 %copy-start.3 = (f32[48,48]{1,0:T(8,128)S(1)}, f32[48,48]{1,0:T(8,128)}, u32[]{:S(2)}) copy-start(f32[48,48]{1,0:T(8,128)} %out_of_ref.1) | copy-start | bytes 27652
  3.3 15.7 %copy-start.4 = (s32[32,2]{0,1:T(2,128)S(1)}, s32[32,2]{0,1:T(2,128)}, u32[]{:S(2)}) copy-start(s32[32,2]{0,1:T(2,128)} %param.9) | copy-start | bytes 772
  3.4 15.7 %copy-start.5 = (f32[48]{0:T(128)S(1)}, f32[48]{0:T(128)}, u32[]{:S(2)}) copy-start(f32[48]{0:T(128)} %param.12) | copy-start | bytes 580
  3.4 15.7 %copy-start.6 = (f32[48]{0:T(128)S(1)}, f32[48]{0:T(128)}, u32[]{:S(2)}) copy-start(f32[48]{0:T(128)} %param.13) | copy-start | bytes 580
  3.4 49.5 %all-to-all-start = ((bf16[256,9,2,128]{3,2,1,0:T(2,128)(2,1)}), bf16[256,9,2,128]{3,2,1,0:T(2,128)(2,1)S(1)}, u32[]{:S(2)}, u32[]{:S(2)}) async-start(bf16[256,9,2,128]{3,2,1,0:T(2,128)(2,1)} %bitcast.22), calls=%async_computation | async-start | bytes 2359296 | tf_op jit(solution)/shard_map/all_to_all | solution.py:391
  19.1 2.2 %copy-start = (bf16[1,16,128,1024]{3,2,1,0:T(8,128)(2,1)S(1)}, bf16[1,16,128,1024]{3,2,1,0:T(8,128)(2,1)}, u32[]{:S(2)}) copy-start(bf16[1,16,128,1024]{3,2,1,0:T(8,128)(2,1)} %param.10) | copy-start | bytes 12582916
